TPU v7x, 32 devices: a whole 2x2x4 slice. The times are simulated.
32 devices in a mesh: ens: 2 (over y), gx: 8 (over z, x), gy: 2 (over core).
Axes of the slice: x: 2, y: 2, z: 4, core: 2. Of those that a mesh axis runs over, the one named last changes fastest.
Arguments:
- right_side: float32 [4, 32, 128, 128], P('ens', 'gx', 'gy'), parts along dimension 0, may hold values from -300 to 300
- cell_diag: float32 [4, 32, 128, 128], P('ens', 'gx', 'gy'), parts along dimension 0, may hold values from 11 to 15
- cell_cross: float32 [4, 32, 128, 128], P('ens', 'gx', 'gy'), parts along dimension 0, may hold values from -1 to 1
- upper_diag: float32 [6, 2, 32, 128, 128], P('ens', None, 'gx', 'gy'), parts along dimension 0, may hold values from 0.2 to 1.2
- upper_cross: float32 [6, 2, 32, 128, 128], P('ens', None, 'gx', 'gy'), parts along dimension 0, may hold values from -0.3 to 0.3
- lower_diag: float32 [6, 2, 32, 128, 128], P('ens', None, 'gx', 'gy'), parts along dimension 0, may hold values from 0.2 to 1.2
- lower_cross: float32 [6, 2, 32, 128, 128], P('ens', None, 'gx', 'gy'), parts along dimension 0, may hold values from -0.3 to 0.3
- spai_diag: float32 [4, 32, 128, 128], P('ens', 'gx', 'gy'), parts along dimension 0, may hold values from 0.06 to 0.1
- spai_cross: float32 [4, 32, 128, 128], P('ens', 'gx', 'gy'), parts along dimension 0, may hold values from -0.03 to 0.03
- perf_cell: int32 [16, 2, 256], P(('ens', 'gx'), 'gy'), parts along dimension 0, may hold values from 0 to 32767, as said below
- perf_owner: int32 [16, 2, 256], P(('ens', 'gx'), 'gy'), parts along dimension 0, may hold values from 0 to 7, as said below
- perf_well: int32 [16, 2, 256], P(('ens', 'gx'), 'gy'), parts along dimension 0, may hold values from 0 to 31
- perf_index: float32 [16, 2, 256], P(('ens', 'gx'), 'gy'), parts along dimension 0, may hold values from 0.5 to 5
- well_storage: float32 [16, 2, 32], P(('ens', 'gx'), 'gy'), parts along dimension 0, may hold values from 2 to 20
Outputs:
- adjoint: float32 [4, 32, 128, 128], P('ens', 'gx', 'gy'), parts along dimension 0
- residual: float32 [4, 32, 128, 128], P('ens', 'gx', 'gy'), parts along dimension 0
There are 2 independent parts, one for each index of `ens`. A program takes and returns all parts, laid end to end along the dimension named above; each array names one. Nothing has to cross between parts.
Inputs may be any that keep to these rules, and one draw needn't show every extreme that they name: `perf_owner`: every perforation's owner lies within two tiles of the perforation's own gx index. Each tile names its own index exactly 128 times and any other owner at most 128 times. `perf_cell`: the perforations of one well lie in one layer and one row of the second dimension, along the first dimension.
All inputs are finite; a program needn't handle non-finite values.
Results may differ from a plain program's by a relative error of at most 0.00024.
Values sent between devices are 32-bit elements; how exact they have to be, the bound alone decides.
A program may use at most 128 MiB of HBM per device.

v0:
```python
import jax
import jax.numpy as jnp
from jax import lax
from jax.sharding import PartitionSpec as P

ITERS = 2


def from_behind(block, axis, distance):
    devices = range(lax.axis_size(axis))
    route = [(i - distance, i) for i in devices if i - distance in devices]
    return lax.ppermute(block, axis, route)


def with_halo(value, sides, width):
    for axis, dim in sides:
        peers, length = (lax.axis_size(axis), value.shape[dim])
        up = [(i, (i + 1) % peers) for i in range(peers - 1)]
        down = [(j, i) for i, j in up]
        last = lax.slice_in_dim(value, length - width, length, axis=dim)
        leading = lax.slice_in_dim(value, 0, width, axis=dim)
        before = lax.ppermute(last, axis, up)
        after = lax.ppermute(leading, axis, down)
        value = jnp.concatenate([before, value, after], axis=dim)
    return value


def transposed(diag, cross, field):
    return jnp.stack(
        [diag[0] * field[0] + cross[1] * field[1], cross[0] * field[0] + diag[1] * field[1]]
    )


def below(field, axis):
    count = field.shape[axis]
    plane = jnp.zeros_like(lax.slice_in_dim(field, 0, 1, axis=axis))
    return jnp.concatenate([plane, lax.slice_in_dim(field, 0, count - 1, axis=axis)], axis=axis)


def above(field, axis):
    count = field.shape[axis]
    plane = jnp.zeros_like(lax.slice_in_dim(field, 0, 1, axis=axis))
    return jnp.concatenate([lax.slice_in_dim(field, 1, count, axis=axis), plane], axis=axis)


def inner(first, second):
    return jnp.sum(first * second)


def send_totals(values, offset):
    return from_behind(values, "gx", offset)


def send_labels(labels, offset):
    return from_behind(labels, "gx", offset)


def send_terms(values, offset):
    return from_behind(values, "gx", offset)


def send_means(values, offset):
    return from_behind(values, "gx", offset)


def shards(
    right_side,
    cell_diag,
    cell_cross,
    upper_diag,
    upper_cross,
    lower_diag,
    lower_cross,
    spai_diag,
    spai_cross,
    perf_cell,
    perf_owner,
    perf_well,
    perf_index,
    well_storage,
):
    cells = perf_cell.reshape(-1)
    owners = perf_owner.reshape(-1)
    wells = perf_well.reshape(-1)
    weights = perf_index.reshape(-1)
    storage = well_storage.reshape(-1)
    owned = storage.shape[0]
    perfs = cells.shape[0]
    reach = (-2, -1, 0, 1, 2)
    position = owners - lax.axis_index("gx") + 2
    bucket_of = position * owned + wells
    local_totals = jax.ops.segment_sum(weights, bucket_of, num_segments=5 * owned).reshape(5, owned)
    totals = local_totals[2]
    for k in range(5):
        if reach[k] != 0:
            totals = totals + send_totals(local_totals[k], reach[k])
    denom = totals + storage
    capacity = perfs // 2
    marks = (position[:, None] == jnp.arange(5, dtype=jnp.int32)[None, :]).astype(jnp.int32)
    ranks = jnp.sum(marks * (jnp.cumsum(marks, axis=0) - 1), axis=1)
    slot = position * capacity + ranks
    labels = jnp.zeros((5 * capacity,), jnp.int32).at[slot].set(wells + 1).reshape(5, capacity)
    arrived = jnp.stack(
        [labels[k] if reach[k] == 0 else send_labels(labels[k], reach[k]) for k in range(5)]
    ).reshape(-1)
    live = arrived > 0
    bucket = jnp.where(live, arrived - 1, owned)
    safe_label = jnp.where(live, arrived - 1, 0)

    def well_means(values):
        buffer = (
            jnp.zeros((2, 5 * capacity), jnp.float32)
            .at[:, slot]
            .set(values)
            .reshape(2, 5, capacity)
        )
        received = jnp.stack(
            [
                buffer[:, k] if reach[k] == 0 else send_terms(buffer[:, k], reach[k])
                for k in range(5)
            ],
            axis=1,
        )
        sums = jax.ops.segment_sum(received.reshape(2, -1).T, bucket, num_segments=owned + 1)[
            :owned
        ]
        means = sums / denom[:, None]
        spread = jnp.where(live[:, None], means[safe_label], 0.0).T.reshape(2, 5, capacity)
        back = jnp.stack(
            [
                spread[:, k] if reach[k] == 0 else send_means(spread[:, k], -reach[k])
                for k in range(5)
            ],
            axis=1,
        )
        return back.reshape(2, -1)[:, slot]

    def well_term(field):
        flat = field.reshape(2, -1)
        values = flat[:, cells]
        means = well_means(weights * values)
        term = weights * (values - means)
        return jnp.zeros_like(flat).at[:, cells].add(term).reshape(field.shape)

    width_x = cell_diag.shape[1]
    width_y = cell_diag.shape[2]
    rim_x = from_behind(
        (upper_diag[0][:, width_x - 1 :], upper_cross[0][:, width_x - 1 :]), "gx", 1
    )
    rim_y = from_behind(
        (upper_diag[1][:, :, width_y - 1 :], upper_cross[1][:, :, width_y - 1 :]), "gy", 1
    )
    prior_x_diag = jnp.concatenate([rim_x[0], upper_diag[0][:, : width_x - 1]], axis=1)
    prior_x_cross = jnp.concatenate([rim_x[1], upper_cross[0][:, : width_x - 1]], axis=1)
    prior_y_diag = jnp.concatenate([rim_y[0], upper_diag[1][:, :, : width_y - 1]], axis=2)
    prior_y_cross = jnp.concatenate([rim_y[1], upper_cross[1][:, :, : width_y - 1]], axis=2)

    def couple(field):
        padded = with_halo(field, (("gx", 1), ("gy", 2)), 1)
        total = transposed(lower_diag[0], lower_cross[0], padded[:, 2:, 1:-1])
        total = total + transposed(prior_x_diag, prior_x_cross, padded[:, :-2, 1:-1])
        total = total + transposed(lower_diag[1], lower_cross[1], padded[:, 1:-1, 2:])
        total = total + transposed(prior_y_diag, prior_y_cross, padded[:, 1:-1, :-2])
        return total

    def apply(field):
        total = couple(field)
        layered = below(transposed(upper_diag[2], upper_cross[2], field), 3)
        layered = layered + transposed(lower_diag[2], lower_cross[2], above(field, 3))
        return transposed(cell_diag, cell_cross, field) - total - layered + well_term(field)

    def precondition(field):
        return transposed(spai_diag, spai_cross, field)

    adjoint = jnp.zeros_like(right_side)
    residual = right_side
    direction = jnp.zeros_like(right_side)
    image = jnp.zeros_like(right_side)
    rho, alpha, omega = (1.0, 1.0, 1.0)
    for step in range(ITERS):
        rho_new = lax.psum(inner(right_side, residual), ("gx", "gy"))
        beta = rho_new / rho * (alpha / omega)
        direction = residual + beta * (direction - omega * image)
        lifted = precondition(direction)
        image = apply(lifted)
        alpha = rho_new / lax.psum(inner(right_side, image), ("gx", "gy"))
        half = residual - alpha * image
        half_lifted = precondition(half)
        turned = apply(half_lifted)
        cross_term, square_term = lax.psum(
            (inner(turned, half), inner(turned, turned)), ("gx", "gy")
        )
        omega = cross_term / square_term
        adjoint = adjoint + alpha * lifted + omega * half_lifted
        residual = half - omega * turned
        rho = rho_new
    return (adjoint, residual)


def solution(mesh):
    in_specs = (
        P("ens", "gx", "gy", None),
        P("ens", "gx", "gy", None),
        P("ens", "gx", "gy", None),
        P("ens", None, "gx", "gy", None),
        P("ens", None, "gx", "gy", None),
        P("ens", None, "gx", "gy", None),
        P("ens", None, "gx", "gy", None),
        P("ens", "gx", "gy", None),
        P("ens", "gx", "gy", None),
        P(("ens", "gx"), "gy", None),
        P(("ens", "gx"), "gy", None),
        P(("ens", "gx"), "gy", None),
        P(("ens", "gx"), "gy", None),
        P(("ens", "gx"), "gy", None),
    )
    out_specs = (P("ens", "gx", "gy", None), P("ens", "gx", "gy", None))
    return jax.shard_map(shards, mesh=mesh, in_specs=in_specs, out_specs=out_specs, check_vma=False)
```

profile of v0, /device:TPU:0, one launch (start us, length us, event | category | flops | bytes accessed | tf_op | source)
XLA Modules:
  0.0 680.0 jit_solution(14436617379083599296)
XLA Ops:
  7.5 5.5 collective-permute-start.10
  27.2 30.1 %psum.56 = f32[]{:T(128)} all-reduce(f32[]{:T(128)} %multiply_reduce_fusion.7), channel_id=1, replica_groups=mesh['ens'=2,'gx'=8,'gy'=2] {'gx','gy'}, use_global_device_ids=true, to_apply=%region_1.0 | all-reduce | flops 1 | bytes 8 | tf_op jit(solution)/shard_map/psum | solution.py:181
  61.7 8.2 %copy.90 = f32[2,32768]{0,1:T(8,128)} copy(f32[2,32768]{1,0:T(2,128)S(1)} %pad_maximum_fusion.4) | data formatting | bytes 524288 | tf_op jit(solution)/shard_map/stack | solution.py:29
  70.6 6.5 gather_fusion
  90.1 5.2 collective-permute-start.14
  101.3 5.4 collective-permute-start.2
  106.8 5.4 collective-permute-start.1
  114.4 6.7 scatter_custom_fusion.2
  145.9 9.5 %scatter_custom_fusion.4 = f32[2,32768]{0,1:T(8,128)} fusion(s32[256]{0:T(256)} %bitcast.456, f32[]{:T(128)} %constant.11.clone.1, f32[256,2]{1,0:T(8,128)S(1)} %gather_fusion, f32[256]{0:T(256)} %bitcast.434, f32[2,640]{0,1:T(8,128)S(1)} %bitcast.430, s32[1024]{0:T(1024)} %get-tuple-element.183), kind=kCustom, calls=%fused_computation.32 | custom fusion | flops 1536 | bytes 274944 | tf_op jit(solution)/shard_map/scatter-add | solution.py:143
  155.4 10.7 %copy.105 = f32[2,4,64,128]{3,2,1,0:T(8,128)} copy(f32[2,4,64,128]{0,3,2,1:T(8,128)} %bitcast.406) | data formatting | bytes 524288 | tf_op jit(solution)/shard_map/reshape | solution.py:143
  182.8 30.1 %psum.57 = f32[]{:T(128)} all-reduce(f32[]{:T(128)} %get-tuple-element.41), channel_id=1, replica_groups=mesh['ens'=2,'gx'=8,'gy'=2] {'gx','gy'}, use_global_device_ids=true, to_apply=%region_11.12 | all-reduce | flops 1 | bytes 8 | tf_op jit(solution)/shard_map/psum | solution.py:186
  216.1 8.2 %copy.106 = f32[2,32768]{0,1:T(8,128)} copy(f32[2,32768]{1,0:T(2,128)S(1)} %pad_maximum_fusion.5) | data formatting | bytes 524288 | tf_op jit(solution)/shard_map/stack | solution.py:29
  224.3 6.6 gather_fusion.2
  253.1 7.0 %scatter_custom_fusion.6 = f32[33,2]{1,0:T(8,128)S(1)} fusion(s32[640]{0:T(1024)} %copy-done.28, f32[640,2]{1,0:T(8,128)} %copy.112, f32[]{:T(128)} %constant.11.clone.1), kind=kCustom, calls=%fused_computation.433 | custom fusion | flops 1280 | bytes 776 | tf_op jit(solution)/shard_map/scatter-add | solution.py:124
  271.9 5.2 collective-permute-start.25
  291.3 10.5 %scatter_custom_fusion.7 = f32[2,32768]{0,1:T(8,128)} fusion(s32[256]{0:T(256)} %bitcast.457, f32[]{:T(128)} %constant.11.clone.1, f32[256,2]{1,0:T(8,128)} %copy-done.18, f32[256]{0:T(256)} %bitcast.435, f32[2,640]{0,1:T(8,128)} %bitcast.431, s32[1024]{0:T(1024)} %get-tuple-element.183), kind=kCustom, calls=%fused_computation.30 | custom fusion | flops 1536 | bytes 726528 | tf_op jit(solution)/shard_map/scatter-add | solution.py:143
  301.8 10.6 %copy.119 = f32[2,4,64,128]{3,2,1,0:T(8,128)} copy(f32[2,4,64,128]{0,3,2,1:T(8,128)} %bitcast.407) | data formatting | bytes 524288 | tf_op jit(solution)/shard_map/reshape | solution.py:143
  325.8 30.1 %all-reduce.9 = (f32[]{:T(128)}, f32[]{:T(128)}) all-reduce(f32[]{:T(128)} %get-tuple-element.5, f32[]{:T(128)} %get-tuple-element.4), channel_id=1, replica_groups=mesh['ens'=2,'gx'=8,'gy'=2] {'gx','gy'}, use_global_device_ids=true, to_apply=%region_16.17 | all-reduce | flops 2 | bytes 16 | tf_op jit(solution)/shard_map/psum | solution.py:190
  360.5 30.1 %psum.60 = f32[]{:T(128)} all-reduce(f32[]{:T(128)} %multiply_reduce_fusion.3), channel_id=1, replica_groups=mesh['ens'=2,'gx'=8,'gy'=2] {'gx','gy'}, use_global_device_ids=true, to_apply=%region_20.21 | all-reduce | flops 1 | bytes 8 | tf_op jit(solution)/shard_map/psum | solution.py:181
  395.1 8.2 %copy.120 = f32[2,32768]{0,1:T(8,128)} copy(f32[2,32768]{1,0:T(2,128)S(1)} %pad_maximum_fusion.6) | data formatting | bytes 524288 | tf_op jit(solution)/shard_map/stack | solution.py:29
  403.3 6.6 gather_fusion.4
  432.0 7.0 %scatter_custom_fusion.9 = f32[33,2]{1,0:T(8,128)S(1)} fusion(s32[640]{0:T(1024)} %copy-done.28, f32[640,2]{1,0:T(8,128)} %copy.126, f32[]{:T(128)} %constant.11.clone.1), kind=kCustom, calls=%fused_computation.431 | custom fusion | flops 1280 | bytes 776 | tf_op jit(solution)/shard_map/scatter-add | solution.py:124
  470.3 10.5 %scatter_custom_fusion.10 = f32[2,32768]{0,1:T(8,128)} fusion(s32[256]{0:T(256)} %bitcast.458, f32[]{:T(128)} %constant.11.clone.1, f32[256,2]{1,0:T(8,128)} %copy-done.19, f32[256]{0:T(256)} %bitcast.436, f32[2,640]{0,1:T(8,128)} %bitcast.432, s32[1024]{0:T(1024)} %get-tuple-element.183), kind=kCustom, calls=%fused_computation.28 | custom fusion | flops 1536 | bytes 726528 | tf_op jit(solution)/shard_map/scatter-add | solution.py:143
  480.7 10.6 %copy.133 = f32[2,4,64,128]{3,2,1,0:T(8,128)} copy(f32[2,4,64,128]{0,3,2,1:T(8,128)} %bitcast.408) | data formatting | bytes 524288 | tf_op jit(solution)/shard_map/reshape | solution.py:143
  505.4 30.1 %psum.61 = f32[]{:T(128)} all-reduce(f32[]{:T(128)} %get-tuple-element.20), channel_id=1, replica_groups=mesh['ens'=2,'gx'=8,'gy'=2] {'gx','gy'}, use_global_device_ids=true, to_apply=%region_25.26 | all-reduce | flops 1 | bytes 8 | tf_op jit(solution)/shard_map/psum | solution.py:186
  540.1 8.2 %copy.134 = f32[2,32768]{0,1:T(8,128)} copy(f32[2,32768]{1,0:T(2,128)S(1)} %pad_maximum_fusion.7) | data formatting | bytes 524288 | tf_op jit(solution)/shard_map/stack | solution.py:29
  548.3 6.6 gather_fusion.6
  574.8 6.8 scatter_custom_fusion.12
  593.5 5.2 collective-permute-start.49
  612.1 10.5 %scatter_custom_fusion.13 = f32[2,32768]{0,1:T(8,128)} fusion(s32[256]{0:T(256)} %bitcast.459, f32[]{:T(128)} %constant.11.clone.1, f32[256,2]{1,0:T(8,128)} %copy-done.17, f32[256]{0:T(256)} %bitcast.437, f32[2,640]{0,1:T(8,128)} %bitcast.429, s32[1024]{0:T(1024)} %get-tuple-element.183), kind=kCustom, calls=%fused_computation.26 | custom fusion | flops 1536 | bytes 726528 | tf_op jit(solution)/shard_map/scatter-add | solution.py:143
  622.6 10.6 %copy.147 = f32[2,4,64,128]{3,2,1,0:T(8,128)} copy(f32[2,4,64,128]{0,3,2,1:T(8,128)} %bitcast.405) | data formatting | bytes 524288 | tf_op jit(solution)/shard_map/reshape | solution.py:143
  646.6 30.1 %all-reduce.8 = (f32[]{:T(128)}, f32[]{:T(128)}) all-reduce(f32[]{:T(128)} %get-tuple-element.3, f32[]{:T(128)} %get-tuple-element.2), channel_id=1, replica_groups=mesh['ens'=2,'gx'=8,'gy'=2] {'gx','gy'}, use_global_device_ids=true, to_apply=%region_30.31 | all-reduce | flops 2 | bytes 16 | tf_op jit(solution)/shard_map/psum | solution.py:190
  (384 shorter events, 284.9 us)
Async XLA Ops:
  4.9 83.9 %collective-permute-start.8 = (s32[128]{0:T(128)S(1)}, s32[128]{0:T(128)S(1)}, u32[]{:S(2)}, u32[]{:S(2)}) collective-permute-start(s32[128]{0:T(128)S(1)} %get-tuple-element.177), channel_id=1, source_target_pairs={{4,0},{6,2},{8,4},{10,6},{12,8},{14,10},{5,1},{7,3},{9,5},{11,7},{... | collective-permute-start | bytes 1544 | tf_op jit(solution)/shard_map/ppermute | solution.py:12
  6.2 83.9 %collective-permute-start.9 = (s32[128]{0:T(128)S(1)}, s32[128]{0:T(128)S(1)}, u32[]{:S(2)}, u32[]{:S(2)}) collective-permute-start(s32[128]{0:T(128)S(1)} %get-tuple-element.176), channel_id=1, source_target_pairs={{2,0},{4,2},{6,4},{8,6},{10,8},{12,10},{14,12},{3,1},{5,3},{7,5},{... | collective-permute-start | bytes 1544 | tf_op jit(solution)/shard_map/ppermute | solution.py:12
  7.5 87.8 %collective-permute-start.10 = (s32[128]{0:T(128)S(1)}, s32[128]{0:T(128)S(1)}, u32[]{:S(2)}, u32[]{:S(2)}) collective-permute-start(s32[128]{0:T(128)S(1)} %get-tuple-element.174), channel_id=1, source_target_pairs={{0,2},{2,4},{4,6},{6,8},{8,10},{10,12},{12,14},{1,3},{3,5},{5,7},{... | collective-permute-start | bytes 1544 | tf_op jit(solution)/shard_map/ppermute | solution.py:12
  15.5 64.7 %collective-permute-start.19 = (f32[32]{0:T(128)S(1)}, f32[32]{0:T(128)S(1)}, u32[]{:S(2)}, u32[]{:S(2)}) collective-permute-start(f32[32]{0:T(128)S(1)} %get-tuple-element.179), channel_id=1, source_target_pairs={{0,4},{2,6},{4,8},{6,10},{8,12},{10,14},{1,5},{3,7},{5,9},{7,11},{... | collective-permute-start | bytes 392 | tf_op jit(solution)/shard_map/ppermute | solution.py:12
  20.2 61.4 %collective-permute-start.18 = (f32[32]{0:T(128)S(1)}, f32[32]{0:T(128)S(1)}, u32[]{:S(2)}, u32[]{:S(2)}) collective-permute-start(f32[32]{0:T(128)S(1)} %get-tuple-element.180), channel_id=1, source_target_pairs={{0,2},{2,4},{4,6},{6,8},{8,10},{10,12},{12,14},{1,3},{3,5},{5,7},{... | collective-permute-start | bytes 392 | tf_op jit(solution)/shard_map/ppermute | solution.py:12
  85.7 14.2 %collective-permute-start.11 = (s32[128]{0:T(128)S(1)}, s32[128]{0:T(128)S(1)}, u32[]{:S(2)}, u32[]{:S(2)}) collective-permute-start(s32[128]{0:T(128)S(1)} %get-tuple-element.173), channel_id=1, source_target_pairs={{0,4},{2,6},{4,8},{6,10},{8,12},{10,14},{1,5},{3,7},{5,9},{7,11},{... | collective-permute-start | bytes 1544 | tf_op jit(solution)/shard_map/ppermute | solution.py:12
  87.4 13.9 %collective-permute-start.12 = (f32[2,128]{1,0:T(2,128)S(1)}, f32[2,128]{1,0:T(2,128)S(1)}, u32[]{:S(2)}, u32[]{:S(2)}) collective-permute-start(f32[2,128]{1,0:T(2,128)S(1)} %bitcast.464), channel_id=1, source_target_pairs={{4,0},{6,2},{8,4},{10,6},{12,8},{14,10},{5,1},{7,3},{9,5},{11,7},{... | collective-permute-start | bytes 3080 | tf_op jit(solution)/shard_map/ppermute | solution.py:12
  88.8 18.0 %collective-permute-start.13 = (f32[2,128]{1,0:T(2,128)S(1)}, f32[2,128]{1,0:T(2,128)S(1)}, u32[]{:S(2)}, u32[]{:S(2)}) collective-permute-start(f32[2,128]{1,0:T(2,128)S(1)} %bitcast.463), channel_id=1, source_target_pairs={{2,0},{4,2},{6,4},{8,6},{10,8},{12,10},{14,12},{3,1},{5,3},{7,5},{... | collective-permute-start | bytes 3080 | tf_op jit(solution)/shard_map/ppermute | solution.py:12
  90.1 22.1 %collective-permute-start.14 = (f32[2,128]{1,0:T(2,128)S(1)}, f32[2,128]{1,0:T(2,128)S(1)}, u32[]{:S(2)}, u32[]{:S(2)}) collective-permute-start(f32[2,128]{1,0:T(2,128)S(1)} %bitcast.462), channel_id=1, source_target_pairs={{0,2},{2,4},{4,6},{6,8},{8,10},{10,12},{12,14},{1,3},{3,5},{5,7},{... | collective-permute-start | bytes 3080 | tf_op jit(solution)/shard_map/ppermute | solution.py:12
  95.3 18.9 %collective-permute-start.15 = (f32[2,128]{1,0:T(2,128)S(1)}, f32[2,128]{1,0:T(2,128)S(1)}, u32[]{:S(2)}, u32[]{:S(2)}) collective-permute-start(f32[2,128]{1,0:T(2,128)S(1)} %bitcast.461), channel_id=1, source_target_pairs={{0,4},{2,6},{4,8},{6,10},{8,12},{10,14},{1,5},{3,7},{5,9},{7,11},{... | collective-permute-start | bytes 3080 | tf_op jit(solution)/shard_map/ppermute | solution.py:12
  99.9 66.2 %collective-permute-start = (f32[2,1,64,128]{3,2,1,0:T(8,128)}, f32[2,1,64,128]{3,2,1,0:T(8,128)S(1)}, u32[]{:S(2)}, u32[]{:S(2)}) collective-permute-start(f32[2,1,64,128]{3,2,1,0:T(8,128)} %get-tuple-element.170), channel_id=1, source_target_pairs={{2,0},{4,2},{6,4},{8,6},{10,8},{12,10},{14,12},{3,1},{5,3},{7,5},{... | collective-permute-start | bytes 196616 | tf_op jit(solution)/shard_map/ppermute | solution.py:23
  101.3 66.1 %collective-permute-start.2 = (f32[2,1,64,128]{3,2,1,0:T(8,128)}, f32[2,1,64,128]{3,2,1,0:T(8,128)S(1)}, u32[]{:S(2)}, u32[]{:S(2)}) collective-permute-start(f32[2,1,64,128]{3,2,1,0:T(8,128)} %get-tuple-element.169), channel_id=1, source_target_pairs={{0,2},{2,4},{4,6},{6,8},{8,10},{10,12},{12,14},{1,3},{3,5},{5,7},{... | collective-permute-start | bytes 196616 | tf_op jit(solution)/shard_map/ppermute | solution.py:22
  106.8 61.9 %collective-permute-start.1 = (f32[2,1,64,128]{3,2,1,0:T(8,128)}, f32[2,1,64,128]{3,2,1,0:T(8,128)}, u32[]{:S(2)}, u32[]{:S(2)}) collective-permute-start(f32[2,1,64,128]{3,2,1,0:T(8,128)} %slice.1005), channel_id=1, source_target_pairs={{0,2},{2,4},{4,6},{6,8},{8,10},{10,12},{12,14},{1,3},{3,5},{5,7},{... | collective-permute-start | bytes 196616 | tf_op jit(solution)/shard_map/ppermute | solution.py:12
  112.2 59.5 %collective-permute-start.3 = (f32[2,1,64,128]{3,2,1,0:T(8,128)}, f32[2,1,64,128]{3,2,1,0:T(8,128)}, u32[]{:S(2)}, u32[]{:S(2)}) collective-permute-start(f32[2,1,64,128]{3,2,1,0:T(8,128)} %slice.1011), channel_id=1, source_target_pairs={{0,2},{2,4},{4,6},{6,8},{8,10},{10,12},{12,14},{1,3},{3,5},{5,7},{... | collective-permute-start | bytes 196616 | tf_op jit(solution)/shard_map/ppermute | solution.py:12
  143.9 33.8 %collective-permute-start.5 = (f32[2,4,1,128]{3,2,1,0:T(1,128)}, f32[2,4,1,128]{3,2,1,0:T(1,128)S(1)}, u32[]{:S(2)}, u32[]{:S(2)}) collective-permute-start(f32[2,4,1,128]{3,2,1,0:T(1,128)} %slice.1015), channel_id=1, source_target_pairs={{0,1},{2,3},{4,5},{6,7},{8,9},{10,11},{12,13},{14,15},{16,17},{18,... | collective-permute-start | bytes 12296 | tf_op jit(solution)/shard_map/ppermute | solution.py:12
  166.1 11.6 %collective-permute-start.7 = (f32[2,4,1,128]{3,2,1,0:T(1,128)S(1)}, f32[2,4,1,128]{3,2,1,0:T(1,128)S(1)}, u32[]{:S(2)}, u32[]{:S(2)}) collective-permute-start(f32[2,4,1,128]{3,2,1,0:T(1,128)S(1)} %copy-done.31), channel_id=1, source_target_pairs={{0,1},{2,3},{4,5},{6,7},{8,9},{10,11},{12,13},{14,15},{16,17},{18,... | collective-permute-start | bytes 12296 | tf_op jit(solution)/shard_map/ppermute | solution.py:12
  235.6 15.1 %collective-permute-start.28 = (f32[2,128]{1,0:T(2,128)S(1)}, f32[2,128]{1,0:T(2,128)}, u32[]{:S(2)}, u32[]{:S(2)}) collective-permute-start(f32[2,128]{1,0:T(2,128)S(1)} %bitcast.480), channel_id=1, source_target_pairs={{4,0},{6,2},{8,4},{10,6},{12,8},{14,10},{5,1},{7,3},{9,5},{11,7},{... | collective-permute-start | bytes 3080 | tf_op jit(solution)/shard_map/ppermute | solution.py:12
  239.3 12.2 %collective-permute-start.29 = (f32[2,128]{1,0:T(2,128)}, f32[2,128]{1,0:T(2,128)}, u32[]{:S(2)}, u32[]{:S(2)}) collective-permute-start(f32[2,128]{1,0:T(2,128)} %bitcast.70), channel_id=1, source_target_pairs={{2,0},{4,2},{6,4},{8,6},{10,8},{12,10},{14,12},{3,1},{5,3},{7,5},{... | collective-permute-start | bytes 3080 | tf_op jit(solution)/shard_map/ppermute | solution.py:12
  241.5 10.6 %collective-permute-start.30 = (f32[2,128]{1,0:T(2,128)S(1)}, f32[2,128]{1,0:T(2,128)S(1)}, u32[]{:S(2)}, u32[]{:S(2)}) collective-permute-start(f32[2,128]{1,0:T(2,128)S(1)} %bitcast.470), channel_id=1, source_target_pairs={{0,2},{2,4},{4,6},{6,8},{8,10},{10,12},{12,14},{1,3},{3,5},{5,7},{... | collective-permute-start | bytes 3080 | tf_op jit(solution)/shard_map/ppermute | solution.py:12
  266.0 18.3 %collective-permute-start.32 = (f32[2,128]{1,0:T(2,128)S(1)}, f32[2,128]{1,0:T(2,128)S(1)}, u32[]{:S(2)}, u32[]{:S(2)}) collective-permute-start(f32[2,128]{1,0:T(2,128)S(1)} %bitcast.466), channel_id=1, source_target_pairs={{0,4},{2,6},{4,8},{6,10},{8,12},{10,14},{1,5},{3,7},{5,9},{7,11},{... | collective-permute-start | bytes 3080 | tf_op jit(solution)/shard_map/ppermute | solution.py:12
  270.6 41.8 %collective-permute-start.24 = (f32[2,1,64,128]{3,2,1,0:T(8,128)}, f32[2,1,64,128]{3,2,1,0:T(8,128)}, u32[]{:S(2)}, u32[]{:S(2)}) collective-permute-start(f32[2,1,64,128]{3,2,1,0:T(8,128)} %get-tuple-element.165), channel_id=1, source_target_pairs={{2,0},{4,2},{6,4},{8,6},{10,8},{12,10},{14,12},{3,1},{5,3},{7,5},{... | collective-permute-start | bytes 196616 | tf_op jit(solution)/shard_map/ppermute | solution.py:23
  271.9 40.6 %collective-permute-start.25 = (f32[2,1,64,128]{3,2,1,0:T(8,128)}, f32[2,1,64,128]{3,2,1,0:T(8,128)}, u32[]{:S(2)}, u32[]{:S(2)}) collective-permute-start(f32[2,1,64,128]{3,2,1,0:T(8,128)} %get-tuple-element.164), channel_id=1, source_target_pairs={{0,2},{2,4},{4,6},{6,8},{8,10},{10,12},{12,14},{1,3},{3,5},{5,7},{... | collective-permute-start | bytes 196616 | tf_op jit(solution)/shard_map/ppermute | solution.py:22
  414.6 15.1 %collective-permute-start.40 = (f32[2,128]{1,0:T(2,128)S(1)}, f32[2,128]{1,0:T(2,128)}, u32[]{:S(2)}, u32[]{:S(2)}) collective-permute-start(f32[2,128]{1,0:T(2,128)S(1)} %bitcast.481), channel_id=1, source_target_pairs={{4,0},{6,2},{8,4},{10,6},{12,8},{14,10},{5,1},{7,3},{9,5},{11,7},{... | collective-permute-start | bytes 3080 | tf_op jit(solution)/shard_map/ppermute | solution.py:12
  418.2 12.1 %collective-permute-start.41 = (f32[2,128]{1,0:T(2,128)}, f32[2,128]{1,0:T(2,128)}, u32[]{:S(2)}, u32[]{:S(2)}) collective-permute-start(f32[2,128]{1,0:T(2,128)} %bitcast.95), channel_id=1, source_target_pairs={{2,0},{4,2},{6,4},{8,6},{10,8},{12,10},{14,12},{3,1},{5,3},{7,5},{... | collective-permute-start | bytes 3080 | tf_op jit(solution)/shard_map/ppermute | solution.py:12
  444.9 18.3 %collective-permute-start.44 = (f32[2,128]{1,0:T(2,128)S(1)}, f32[2,128]{1,0:T(2,128)S(1)}, u32[]{:S(2)}, u32[]{:S(2)}) collective-permute-start(f32[2,128]{1,0:T(2,128)S(1)} %bitcast.467), channel_id=1, source_target_pairs={{0,4},{2,6},{4,8},{6,10},{8,12},{10,14},{1,5},{3,7},{5,9},{7,11},{... | collective-permute-start | bytes 3080 | tf_op jit(solution)/shard_map/ppermute | solution.py:12
  449.5 41.9 %collective-permute-start.36 = (f32[2,1,64,128]{3,2,1,0:T(8,128)}, f32[2,1,64,128]{3,2,1,0:T(8,128)}, u32[]{:S(2)}, u32[]{:S(2)}) collective-permute-start(f32[2,1,64,128]{3,2,1,0:T(8,128)} %get-tuple-element.160), channel_id=1, source_target_pairs={{2,0},{4,2},{6,4},{8,6},{10,8},{12,10},{14,12},{3,1},{5,3},{7,5},{... | collective-permute-start | bytes 196616 | tf_op jit(solution)/shard_map/ppermute | solution.py:23
  450.8 40.6 %collective-permute-start.37 = (f32[2,1,64,128]{3,2,1,0:T(8,128)}, f32[2,1,64,128]{3,2,1,0:T(8,128)}, u32[]{:S(2)}, u32[]{:S(2)}) collective-permute-start(f32[2,1,64,128]{3,2,1,0:T(8,128)} %get-tuple-element.159), channel_id=1, source_target_pairs={{0,2},{2,4},{4,6},{6,8},{8,10},{10,12},{12,14},{1,3},{3,5},{5,7},{... | collective-permute-start | bytes 196616 | tf_op jit(solution)/shard_map/ppermute | solution.py:22
  558.0 15.4 %collective-permute-start.52 = (f32[2,128]{1,0:T(2,128)S(1)}, f32[2,128]{1,0:T(2,128)S(1)}, u32[]{:S(2)}, u32[]{:S(2)}) collective-permute-start(f32[2,128]{1,0:T(2,128)S(1)} %bitcast.482), channel_id=1, source_target_pairs={{4,0},{6,2},{8,4},{10,6},{12,8},{14,10},{5,1},{7,3},{9,5},{11,7},{... | collective-permute-start | bytes 3080 | tf_op jit(solution)/shard_map/ppermute | solution.py:12
  561.0 12.3 %collective-permute-start.53 = (f32[2,128]{1,0:T(2,128)S(1)}, f32[2,128]{1,0:T(2,128)S(1)}, u32[]{:S(2)}, u32[]{:S(2)}) collective-permute-start(f32[2,128]{1,0:T(2,128)S(1)} %bitcast.483), channel_id=1, source_target_pairs={{2,0},{4,2},{6,4},{8,6},{10,8},{12,10},{14,12},{3,1},{5,3},{7,5},{... | collective-permute-start | bytes 3080 | tf_op jit(solution)/shard_map/ppermute | solution.py:12
  587.5 17.5 %collective-permute-start.56 = (f32[2,128]{1,0:T(2,128)S(1)}, f32[2,128]{1,0:T(2,128)S(1)}, u32[]{:S(2)}, u32[]{:S(2)}) collective-permute-start(f32[2,128]{1,0:T(2,128)S(1)} %bitcast.468), channel_id=1, source_target_pairs={{0,4},{2,6},{4,8},{6,10},{8,12},{10,14},{1,5},{3,7},{5,9},{7,11},{... | collective-permute-start | bytes 3080 | tf_op jit(solution)/shard_map/ppermute | solution.py:12
  592.2 41.0 %collective-permute-start.48 = (f32[2,1,64,128]{3,2,1,0:T(8,128)}, f32[2,1,64,128]{3,2,1,0:T(8,128)}, u32[]{:S(2)}, u32[]{:S(2)}) collective-permute-start(f32[2,1,64,128]{3,2,1,0:T(8,128)} %get-tuple-element.155), channel_id=1, source_target_pairs={{2,0},{4,2},{6,4},{8,6},{10,8},{12,10},{14,12},{3,1},{5,3},{7,5},{... | collective-permute-start | bytes 196616 | tf_op jit(solution)/shard_map/ppermute | solution.py:23
  593.5 39.7 %collective-permute-start.49 = (f32[2,1,64,128]{3,2,1,0:T(8,128)}, f32[2,1,64,128]{3,2,1,0:T(8,128)}, u32[]{:S(2)}, u32[]{:S(2)}) collective-permute-start(f32[2,1,64,128]{3,2,1,0:T(8,128)} %get-tuple-element.154), channel_id=1, source_target_pairs={{0,2},{2,4},{4,6},{6,8},{8,10},{10,12},{12,14},{1,3},{3,5},{5,7},{... | collective-permute-start | bytes 196616 | tf_op jit(solution)/shard_map/ppermute | solution.py:22
  (63 other events, 1698.5 us)
where the time goes:
time: 692 us; the launch traced here: 680 us
  blocking collectives  181 us (26%)
  local copies, waits for them, and re-layouts  158 us (23%)
  starting transfers between devices  158 us (23%)
  other arithmetic  147 us (21%)
  waiting for transfers between devices  23.9 us (3%)
  between operations  12.3 us (2%)
    ppermute x44, starting transfers between devices, from_behind(): return lax.ppermute(block, axis, route)  115 us
    psum x2, blocking collectives, shards(): alpha = rho_new / lax.psum(inner(right_side, image), ('gx', 'gy'))  60.2 us
    psum x2, blocking collectives, shards(): lax.psum((inner(turned, half), inner(turned, turned)), ('gx', 'gy'))  60.2 us
    psum x2, blocking collectives, shards(): rho_new = lax.psum(inner(right_side, residual), ('gx', 'gy'))  60.2 us
    reshape x4, local copies, waits for them, and re-layouts, well_term(): return jnp.zeros_like(flat).at[:, cells].add(term).reshape(field.shape)  42.5 us
    scatter-add x4, other arithmetic, well_term(): return jnp.zeros_like(flat).at[:, cells].add(term).reshape(field.shape)  40.9 us
    ppermute x8, starting transfers between devices, with_halo(): before = lax.ppermute(last, axis, up)  33.1 us
    another operation x4, local copies, waits for them, and re-layouts, transposed(): jnp.stack([diag[0] * field[0] + cross[1] * field[1], cross[0] * field[0]...  32.9 us
  transfers between devices with their start and end apart: 60, of which 11 were waited for; matrix products, arithmetic and copies ran while one was open for 25% of the time, Pallas kernels for 0%

commit v1 on v0

v1 whole, which is shorter than its diff:
```python
import functools

import jax
import jax.numpy as jnp
from jax import lax
from jax.experimental import pallas as pl
from jax.experimental.pallas import tpu as pltpu
from jax.sharding import PartitionSpec as P

MESH = pl.DeviceIdType.MESH
ITERS = 2
POWERS = 2 * ITERS
SHIFT = 1.0
RING = 8
REACH = 4
F32 = jnp.float32
BF16 = jnp.bfloat16


def parts(value, count):
    pieces = []
    for _ in range(count):
        piece = value.astype(BF16)
        pieces.append(piece)
        value = value - piece.astype(F32)
    return pieces


def rows_dot(first, second):
    return lax.dot_general(first, second, (((1,), (1,)), ((), ())), preferred_element_type=F32)


def combine(terms, vectors):
    total = None
    for term, vector in zip(terms, vectors):
        if term is None:
            continue
        piece = term * vector
        total = piece if total is None else total + piece
    return total


def add(first, second):
    if first is None:
        return second
    if second is None:
        return first
    return first + second


def scale(factor, terms):
    return [None if t is None else factor * t for t in terms]


def plus(first, second):
    return [add(a, b) for a, b in zip(first, second)]


def advance(terms):
    moved = [None] + list(terms[:-1])
    return plus(moved, scale(SHIFT, terms))


def bicgstab_terms(gram):
    def product(first, second):
        total = None
        for i, a in enumerate(first):
            for j, b in enumerate(second):
                if a is not None and b is not None:
                    total = add(total, a * b * gram[(min(i, j), max(i, j))])
        return total

    count = POWERS + 1
    one = jnp.ones_like(gram[(0, 0)])
    shadow = [one] + [None] * (count - 1)
    residual = list(shadow)
    adjoint = [None] * count
    direction = image = None
    rho = alpha = omega = one
    for step in range(ITERS):
        rho_new = product(shadow, residual)
        if step == 0:
            direction = residual
        else:
            beta = rho_new / rho * (alpha / omega)
            direction = plus(residual, scale(beta, plus(direction, scale(-omega, image))))
        image = advance(direction)
        alpha = rho_new / product(shadow, image)
        half = plus(residual, scale(-alpha, image))
        turned = advance(half)
        omega = product(turned, half) / product(turned, turned)
        adjoint = plus(adjoint, plus(scale(alpha, direction), scale(omega, half)))
        residual = plus(half, scale(-omega, turned))
        rho = rho_new
    return adjoint, residual


def kernel(
    peers,
    rhs,
    cell_diag,
    cell_cross,
    up_diag,
    up_cross,
    low_diag,
    low_cross,
    spai_diag,
    spai_cross,
    perf_cell,
    perf_owner,
    perf_well,
    perf_index,
    storage,
    adjoint_out,
    residual_out,
    basis,
    lifted,
    diag,
    spread,
    mask,
    denom,
    totals,
    up_send,
    up_recv,
    down_recv,
    y_send,
    y_recv,
    well_send,
    well_recv,
    dots,
    dots_all,
    halo_send_sem,
    halo_recv_sem,
    well_send_sem,
    well_recv_sem,
    dots_send_sem,
    dots_recv_sem,
):
    gx, gy = lax.axis_index("gx"), lax.axis_index("gy")
    everyone = peers * 2
    me = gx * 2 + gy
    _, width, height, depth = rhs.shape
    rows = width * height
    lanes = perf_cell.shape[-1]
    owned = storage.shape[-1]
    buckets = RING * owned

    well_recv[...] = jnp.zeros_like(well_recv)
    barrier = pltpu.get_barrier_semaphore()
    for step in range(1, everyone):
        other = lax.rem(me + step, everyone)
        pl.semaphore_signal(
            barrier, 1, device_id={"gx": other // 2, "gy": other % 2}, device_id_type=MESH
        )

    cells = perf_cell[0]
    bucket_of = (perf_owner[0] & (RING - 1)) * owned + perf_well[0]
    row_of, layer_of = (cells // depth, cells % depth)
    weights = perf_index[0]
    in_row = lax.broadcasted_iota(jnp.int32, (rows, lanes), 0) == row_of
    in_bucket = lax.broadcasted_iota(jnp.int32, (buckets, lanes), 0) == bucket_of
    in_layer = lax.broadcasted_iota(jnp.int32, (depth, lanes), 0) == layer_of
    hot_row = in_row.astype(F32).astype(BF16)
    hot_bucket = in_bucket.astype(F32).astype(BF16)
    hot_layer = in_layer.astype(F32).astype(BF16)
    spread_now = jnp.zeros((rows, buckets), F32)
    extra = jnp.zeros((rows, depth), F32)
    for piece in parts(weights, 3):
        piece = piece.astype(F32)
        spread_now += rows_dot(hot_row, jnp.where(in_bucket, piece, 0.0).astype(BF16))
        extra += rows_dot(hot_row, jnp.where(in_layer, piece, 0.0).astype(BF16))
    spread[...] = spread_now
    layer_of_bucket = jnp.minimum(rows_dot(hot_bucket, hot_layer), 1.0).astype(BF16)
    bucket_of_layer = jnp.minimum(rows_dot(hot_layer, hot_bucket), 1.0).astype(BF16)
    layer_twice = jnp.concatenate([layer_of_bucket, layer_of_bucket], axis=0)
    bucket_twice = jnp.concatenate([bucket_of_layer, bucket_of_layer], axis=0)
    for c in range(2):
        for x in range(width):
            diag[c, x] = cell_diag[c, x] + extra[x * height : (x + 1) * height]

    place = lax.broadcasted_iota(jnp.int32, (owned, buckets), 1)
    slot = lax.broadcasted_iota(jnp.int32, (owned, buckets), 0)
    mine = (place // owned == (gx & (RING - 1))) & (place % owned == slot)
    stored = jnp.zeros((8, buckets), F32)
    for piece in parts(jnp.broadcast_to(storage[0], (8, owned)), 3):
        stored += jnp.dot(piece, mine.astype(F32).astype(BF16), preferred_element_type=F32)
    weight_sums = jnp.sum(spread_now, axis=0, keepdims=True) + stored[:1]

    tile_row = lax.broadcasted_iota(jnp.int32, (8, 128), 0)
    tile_lane = lax.broadcasted_iota(jnp.int32, (8, 128), 1)
    residue = ((tile_row % 2) * 128 + tile_lane) // owned
    here = (residue - gx + 2) & (RING - 1)
    for k in range(2 * REACH + 1):
        away = k - REACH
        there = (residue - gx - away + 2) & (RING - 1)
        same = (here < 5) & (there < 5) & (here == there + away)
        mask[k] = same.astype(F32)

    lane = lax.broadcasted_iota(jnp.int32, (height, depth), 1)
    row = lax.broadcasted_iota(jnp.int32, (height, depth), 0)
    first_lane, last_lane = (lane == 0, lane == depth - 1)
    first_row, last_row = (row == 0, row == height - 1)

    pl.semaphore_wait(barrier, everyone - 1)

    def vector(k):
        return rhs if k == 0 else basis.at[k - 1]

    def start_wells(step):
        for k in range(2 * REACH + 1):
            if k == REACH:
                continue
            away = REACH - k

            @pl.when((gx + away >= 0) & (gx + away < peers))
            def _():
                pltpu.make_async_remote_copy(
                    src_ref=well_send.at[step],
                    dst_ref=well_recv.at[step, k],
                    send_sem=well_send_sem.at[step, k],
                    recv_sem=well_recv_sem.at[step, k],
                    device_id={"gx": gx + away},
                    device_id_type=MESH,
                ).start()

    def well_copy(step, k):
        return pltpu.make_async_remote_copy(
            src_ref=well_send.at[step],
            dst_ref=well_recv.at[step, k],
            send_sem=well_send_sem.at[step, k],
            recv_sem=well_recv_sem.at[step, k],
            device_id={"gx": gx},
            device_id_type=MESH,
        )

    def halo_copy(step, kind):
        src, dst, target = [
            (up_send.at[step], up_recv.at[step], {"gx": gx + 1}),
            (lifted.at[step, :, 0], down_recv.at[step], {"gx": gx - 1}),
            (y_send.at[step], y_recv.at[step], {"gy": 1 - gy}),
        ][kind]
        return pltpu.make_async_remote_copy(
            src_ref=src,
            dst_ref=dst,
            send_sem=halo_send_sem.at[step, kind],
            recv_sem=halo_recv_sem.at[step, kind],
            device_id=target,
            device_id_type=MESH,
        )

    def block(diag_ref, cross_ref, at, f0, f1):
        d0, d1 = (diag_ref[(*at[0], 0, *at[1])], diag_ref[(*at[0], 1, *at[1])])
        c0, c1 = (cross_ref[(*at[0], 0, *at[1])], cross_ref[(*at[0], 1, *at[1])])
        return (d0 * f0 + c1 * f1, c0 * f0 + d1 * f1)

    def add_dots(k):
        sums = [jnp.zeros((8, depth), F32) for _ in range(k + 1)]
        for c in range(2):
            for x in range(width):
                last = vector(k)[c, x]
                for j in range(k + 1):
                    other = last if j == k else vector(j)[c, x]
                    sums[j] += jnp.sum((last * other).reshape(height // 8, 8, depth), axis=0)
        for j in range(k + 1):
            at = k * (k + 1) // 2 + j
            dots[at : at + 1, :] = jnp.sum(sums[j], axis=0, keepdims=True)

    for step in range(POWERS):
        source = vector(step)

        def lift(x):
            f0, f1 = block(spai_diag, spai_cross, ((), (x,)), source[0, x], source[1, x])
            lifted[step, 0, x] = f0
            lifted[step, 1, x] = f1
            return f0, f1

        lift(0)

        @pl.when(gx > 0)
        def _():
            halo_copy(step, 1).start()

        f0, f1 = lift(width - 1)
        p0, p1 = block(up_diag, up_cross, ((0,), (width - 1,)), f0, f1)
        up_send[step, 0] = p0
        up_send[step, 1] = p1

        @pl.when(gx < peers - 1)
        def _():
            halo_copy(step, 0).start()

        for x in range(1, width - 1):
            lift(x)

        @pl.when(gy == 0)
        def _():
            at = slice(height - 1, height)
            for x in range(width):
                p0, p1 = block(
                    up_diag,
                    up_cross,
                    ((1,), (x, at)),
                    lifted[step, 0, x, at],
                    lifted[step, 1, x, at],
                )
                y_send[step, x : x + 1] = p0
                y_send[step, width + x : width + x + 1] = p1

        @pl.when(gy == 1)
        def _():
            for x in range(width):
                for c in range(2):
                    y_send[step, c * width + x : c * width + x + 1] = lifted[step, c, x, 0:1]

        halo_copy(step, 2).start()

        for c in range(2):
            field = lifted[step, c].reshape(rows, depth)
            picked = jnp.dot(
                jnp.concatenate(parts(field, 2), axis=1),
                bucket_twice,
                preferred_element_type=F32,
            )
            sums = jnp.sum(picked * spread[...], axis=0, keepdims=True)
            well_send[step, 2 * c : 2 * c + 1] = sums[:, :128]
            well_send[step, 2 * c + 1 : 2 * c + 2] = sums[:, 128:]
        well_send[step, 4:5] = weight_sums[:, :128]
        well_send[step, 5:6] = weight_sums[:, 128:]
        well_send[step, 6:8] = jnp.zeros((2, 128), F32)
        start_wells(step)

        carry = None
        for x in range(width):
            f0, f1 = (lifted[step, 0, x], lifted[step, 1, x])
            here = ((), (x,))
            a0, a1 = block(diag, cell_cross, here, f0, f1)
            a0 -= SHIFT * source[0, x]
            a1 -= SHIFT * source[1, x]
            if carry is not None:
                a0 -= carry[0]
                a1 -= carry[1]
            if x < width - 1:
                carry = block(up_diag, up_cross, ((0,), (x,)), f0, f1)
                b0, b1 = block(
                    low_diag, low_cross, ((0,), (x,)), lifted[step, 0, x + 1], lifted[step, 1, x + 1]
                )
                a0 -= b0
                a1 -= b1
            y_up = block(up_diag, up_cross, ((1,), (x,)), f0, f1)
            a0 -= jnp.where(first_row, 0.0, pltpu.roll(y_up[0], 1, 0))
            a1 -= jnp.where(first_row, 0.0, pltpu.roll(y_up[1], 1, 0))
            next0 = jnp.where(last_row, 0.0, pltpu.roll(f0, height - 1, 0))
            next1 = jnp.where(last_row, 0.0, pltpu.roll(f1, height - 1, 0))
            b0, b1 = block(low_diag, low_cross, ((1,), (x,)), next0, next1)
            a0 -= b0
            a1 -= b1
            z_up = block(up_diag, up_cross, ((2,), (x,)), f0, f1)
            a0 -= jnp.where(first_lane, 0.0, pltpu.roll(z_up[0], 1, 1))
            a1 -= jnp.where(first_lane, 0.0, pltpu.roll(z_up[1], 1, 1))
            next0 = jnp.where(last_lane, 0.0, pltpu.roll(f0, depth - 1, 1))
            next1 = jnp.where(last_lane, 0.0, pltpu.roll(f1, depth - 1, 1))
            b0, b1 = block(low_diag, low_cross, ((2,), (x,)), next0, next1)
            basis[step, 0, x] = a0 - b0
            basis[step, 1, x] = a1 - b1
        add_dots(step)

        for k in range(2 * REACH + 1):
            if k == REACH:
                continue
            away = k - REACH

            @pl.when((gx + away >= 0) & (gx + away < peers))
            def _():
                well_copy(step, k).wait_recv()

        total = well_send[step]
        for k in range(2 * REACH + 1):
            if k != REACH:
                total += mask[k] * well_recv[step, k]
        if step == 0:
            totals[...] = total
            for r in range(4):
                below = totals[4 + r % 2 : 5 + r % 2]
                denom[r : r + 1] = jnp.where(below > 0.0, below, 1.0)
        means = total[:4] / denom[...]
        for c in range(2):
            mean = jnp.concatenate([means[2 * c : 2 * c + 1], means[2 * c + 1 : 2 * c + 2]], axis=1)
            taken = jnp.concatenate(parts(mean * spread[...], 2), axis=1)
            taken = jnp.dot(taken, layer_twice, preferred_element_type=F32)
            for x in range(width):
                basis[step, c, x] -= taken[x * height : (x + 1) * height]

        halo_copy(step, 2).wait_recv()

        @pl.when(gy == 0)
        def _():
            at = slice(height - 1, height)
            for x in range(width):
                f0, f1 = (y_recv[step, x : x + 1], y_recv[step, width + x : width + x + 1])
                b0, b1 = block(low_diag, low_cross, ((1,), (x, at)), f0, f1)
                basis[step, 0, x, at] -= b0
                basis[step, 1, x, at] -= b1

        @pl.when(gy == 1)
        def _():
            for x in range(width):
                for c in range(2):
                    at = c * width + x
                    basis[step, c, x, 0:1] -= y_recv[step, at : at + 1]

        @pl.when(gx > 0)
        def _():
            halo_copy(step, 0).wait_recv()
            for c in range(2):
                basis[step, c, 0] -= up_recv[step, c]

        @pl.when(gx < peers - 1)
        def _():
            halo_copy(step, 1).wait_recv()
            x = width - 1
            f0, f1 = (down_recv[step, 0], down_recv[step, 1])
            b0, b1 = block(low_diag, low_cross, ((0,), (x,)), f0, f1)
            basis[step, 0, x] -= b0
            basis[step, 1, x] -= b1

    add_dots(POWERS)
    dots[15:16, :] = jnp.zeros((1, depth), F32)

    def dots_copy(index, other):
        return pltpu.make_async_remote_copy(
            src_ref=dots,
            dst_ref=dots_all.at[index],
            send_sem=dots_send_sem.at[index],
            recv_sem=dots_recv_sem.at[index],
            device_id={"gx": other // 2, "gy": other % 2},
            device_id_type=MESH,
        )

    for step in range(1, everyone):
        other = lax.rem(me + step, everyone)
        pltpu.make_async_remote_copy(
            src_ref=dots,
            dst_ref=dots_all.at[me],
            send_sem=dots_send_sem.at[step],
            recv_sem=dots_recv_sem.at[me],
            device_id={"gx": other // 2, "gy": other % 2},
            device_id_type=MESH,
        ).start()
    dots_all[me] = dots[...]
    for step in range(1, everyone):
        other = lax.rem(me + step, everyone)
        dots_copy(other, other).wait_recv()
    gathered = jnp.sum(dots_all[...], axis=0)
    gathered = jnp.broadcast_to(jnp.sum(gathered, axis=1, keepdims=True), gathered.shape)
    gram = {}
    for k in range(POWERS + 1):
        for j in range(k + 1):
            at = k * (k + 1) // 2 + j
            gram[(j, k)] = gathered[at : at + 1, :]
    adjoint, residual = bicgstab_terms(gram)

    for x in range(width):
        fields = []
        for c in range(2):
            values = [vector(k)[c, x] for k in range(POWERS + 1)]
            residual_out[c, x] = combine(residual, values)
            fields.append(combine(adjoint, values))
        f0, f1 = block(spai_diag, spai_cross, ((), (x,)), *fields)
        adjoint_out[0, x] = f0
        adjoint_out[1, x] = f1

    for step in range(POWERS):

        @pl.when(gx < peers - 1)
        def _():
            halo_copy(step, 0).wait_send()

        @pl.when(gx > 0)
        def _():
            halo_copy(step, 1).wait_send()

        halo_copy(step, 2).wait_send()
        for k in range(2 * REACH + 1):
            if k == REACH:
                continue
            away = REACH - k

            @pl.when((gx + away >= 0) & (gx + away < peers))
            def _():
                well_copy(step, k).wait_send()

    for step in range(1, everyone):
        dots_copy(step, me).wait_send()


def shards(peers, *args):
    rhs = args[0]
    _, width, height, depth = rhs.shape
    owned = args[-1].shape[-1]
    buckets = RING * owned
    rows = width * height
    everyone = peers * 2
    plane = (POWERS, 2, height, depth)
    wells = 2 * REACH + 1
    vmem = pl.BlockSpec(memory_space=pltpu.VMEM)
    return pl.pallas_call(
        functools.partial(kernel, peers),
        out_shape=[jax.ShapeDtypeStruct(rhs.shape, F32)] * 2,
        in_specs=[vmem] * len(args),
        out_specs=[vmem] * 2,
        scratch_shapes=[
            pltpu.VMEM((POWERS, 2, width, height, depth), F32),
            pltpu.VMEM((POWERS, 2, width, height, depth), F32),
            pltpu.VMEM((2, width, height, depth), F32),
            pltpu.VMEM((rows, buckets), F32),
            pltpu.VMEM((wells, 8, 128), F32),
            pltpu.VMEM((4, 128), F32),
            pltpu.VMEM((8, 128), F32),
            pltpu.VMEM(plane, F32),
            pltpu.VMEM(plane, F32),
            pltpu.VMEM(plane, F32),
            pltpu.VMEM((POWERS, 2 * width, depth), F32),
            pltpu.VMEM((POWERS, 2 * width, depth), F32),
            pltpu.VMEM((POWERS, 8, 128), F32),
            pltpu.VMEM((POWERS, wells, 8, 128), F32),
            pltpu.VMEM((16, depth), F32),
            pltpu.VMEM((everyone, 16, depth), F32),
            pltpu.SemaphoreType.DMA((POWERS, 3)),
            pltpu.SemaphoreType.DMA((POWERS, 3)),
            pltpu.SemaphoreType.DMA((POWERS, wells)),
            pltpu.SemaphoreType.DMA((POWERS, wells)),
            pltpu.SemaphoreType.DMA((everyone,)),
            pltpu.SemaphoreType.DMA((everyone,)),
        ],
        compiler_params=pltpu.CompilerParams(
            collective_id=0, has_side_effects=True, vmem_limit_bytes=40 * 1024 * 1024
        ),
    )(*args)


def solution(mesh):
    cell = P("ens", "gx", "gy", None)
    coupling = P("ens", None, "gx", "gy", None)
    tile = P(("ens", "gx"), "gy", None)
    in_specs = (cell,) * 3 + (coupling,) * 4 + (cell,) * 2 + (tile,) * 5
    return jax.shard_map(
        functools.partial(shards, mesh.shape["gx"]),
        mesh=mesh,
        in_specs=in_specs,
        out_specs=(cell, cell),
        check_vma=False,
    )
```

time: 692 us -> 46.3 us (0.07); the launches traced: 680 us -> 45.8 us
  blocking collectives: 181 us -> 0 us
  starting transfers between devices: 158 us -> 0 us
  other arithmetic: 147 us -> 0 us
  local copies, waits for them, and re-layouts: 158 us -> 14 us
  Pallas kernels: 0 us -> 31.1 us
  waiting for transfers between devices: 23.9 us -> 0 us
  between operations: 12.3 us -> 0.67 us
    psum x6 -> x0, blocking collectives: 181 us -> none  [the longest x2 60.2 us: shards(): alpha = rho_new / lax.psum(inner(right_side, image), ('gx', 'gy'))]
    ppermute x60 -> x0, starting transfers between devices: 158 us -> none  [the longest x44 115 us: from_behind(): return lax.ppermute(block, axis, route)]
    scatter-add x9 -> x0, other arithmetic: 70.9 us -> none  [the longest x4 40.9 us: well_term(): return jnp.zeros_like(flat).at[:, cells].add(term).reshape(field.shape)]
    reshape x4 -> x0, local copies, waits for them, and re-layouts: 42.5 us -> none  [well_term(): return jnp.zeros_like(flat).at[:, cells].add(term).reshape(field.shape)]
    add x34 -> x0, other arithmetic: 39.2 us -> none  [the longest x24 29.2 us: transposed(): diag[0] * field[0] + cross[1] * field[1]]
    another operation x19 -> x0, local copies, waits for them, and re-layouts: 36 us -> none  [the longest x4 32.9 us: transposed(): jnp.stack([diag[0] * field[0] + cross[1] * field[1], cross[0] * field[0]...]
    gather x8 -> x0, local copies, waits for them, and re-layouts: 35.3 us -> none  [the longest x4 26.4 us: well_term(): values = flat[:, cells]]
    pallas_call x0 -> x1, Pallas kernels: none -> 31.1 us  [shards(): pl.pallas_call(functools.partial(kernel, peers), out_shape=[jax.ShapeDtyp...]
  transfers between devices with their start and end apart: 60 -> 0, of which waited for: 11 -> 0; matrix products, arithmetic and copies ran while one was open for 25% -> 0% of each run, Pallas kernels for 0% -> 0%
where the time goes in v1:
time: 46.3 us; the launch traced here: 45.8 us
  Pallas kernels  31.1 us (67%)
  local copies, waits for them, and re-layouts  14 us (30%)
  between operations  0.67 us (1%)
    pallas_call x1, Pallas kernels, shards(): pl.pallas_call(functools.partial(kernel, peers), out_shape=[jax.ShapeDtyp...  31.1 us
    unnamed x30, local copies, waits for them, and re-layouts  14 us

profile of v1, /device:TPU:0, one launch (start us, length us, event | category | flops | bytes accessed | tf_op | source)
XLA Modules:
  0.0 45.8 jit_solution(8323941798596813425)
XLA Ops:
  0.6 0.0 copy-start
  0.6 1.1 %copy-done = f32[3,2,4,64,128]{4,3,2,1,0:T(8,128)S(1)} copy-done((f32[3,2,4,64,128]{4,3,2,1,0:T(8,128)S(1)}, f32[3,2,4,64,128]{4,3,2,1,0:T(8,128)}, u32[]{:S(2)}) %copy-start) | copy-done | bytes 786456
  1.8 0.0 copy-start.1
  1.8 1.1 %copy-done.1 = f32[3,2,4,64,128]{4,3,2,1,0:T(8,128)S(1)} copy-done((f32[3,2,4,64,128]{4,3,2,1,0:T(8,128)S(1)}, f32[3,2,4,64,128]{4,3,2,1,0:T(8,128)}, u32[]{:S(2)}) %copy-start.1) | copy-done | bytes 786456
  2.9 0.0 copy-start.2
  2.9 1.1 %copy-done.2 = f32[3,2,4,64,128]{4,3,2,1,0:T(8,128)S(1)} copy-done((f32[3,2,4,64,128]{4,3,2,1,0:T(8,128)S(1)}, f32[3,2,4,64,128]{4,3,2,1,0:T(8,128)}, u32[]{:S(2)}) %copy-start.2) | copy-done | bytes 786456
  4.0 0.0 copy-start.3
  4.0 1.1 %copy-done.3 = f32[3,2,4,64,128]{4,3,2,1,0:T(8,128)S(1)} copy-done((f32[3,2,4,64,128]{4,3,2,1,0:T(8,128)S(1)}, f32[3,2,4,64,128]{4,3,2,1,0:T(8,128)}, u32[]{:S(2)}) %copy-start.3) | copy-done | bytes 786456
  5.2 0.0 copy-start.4
  5.2 0.9 %copy-done.4 = f32[2,4,64,128]{3,2,1,0:T(8,128)S(1)} copy-done((f32[2,4,64,128]{3,2,1,0:T(8,128)S(1)}, f32[2,4,64,128]{3,2,1,0:T(8,128)}, u32[]{:S(2)}) %copy-start.4) | copy-done | bytes 262168
  6.1 0.0 copy-start.5
  6.1 0.9 %copy-done.5 = f32[2,4,64,128]{3,2,1,0:T(8,128)S(1)} copy-done((f32[2,4,64,128]{3,2,1,0:T(8,128)S(1)}, f32[2,4,64,128]{3,2,1,0:T(8,128)}, u32[]{:S(2)}) %copy-start.5) | copy-done | bytes 262168
  7.1 0.0 copy-start.6
  7.1 0.9 %copy-done.6 = f32[2,4,64,128]{3,2,1,0:T(8,128)S(1)} copy-done((f32[2,4,64,128]{3,2,1,0:T(8,128)S(1)}, f32[2,4,64,128]{3,2,1,0:T(8,128)}, u32[]{:S(2)}) %copy-start.6) | copy-done | bytes 262168
  8.0 0.0 copy-start.7
  8.0 0.9 %copy-done.7 = f32[2,4,64,128]{3,2,1,0:T(8,128)S(1)} copy-done((f32[2,4,64,128]{3,2,1,0:T(8,128)S(1)}, f32[2,4,64,128]{3,2,1,0:T(8,128)}, u32[]{:S(2)}) %copy-start.7) | copy-done | bytes 262168
  9.0 0.0 copy-start.8
  9.0 0.9 %copy-done.8 = f32[2,4,64,128]{3,2,1,0:T(8,128)S(1)} copy-done((f32[2,4,64,128]{3,2,1,0:T(8,128)S(1)}, f32[2,4,64,128]{3,2,1,0:T(8,128)}, u32[]{:S(2)}) %copy-start.8) | copy-done | bytes 262168
  9.9 0.0 copy-start.9
  9.9 0.7 %copy-done.9 = s32[1,1,256]{2,1,0:T(1,128)S(1)} copy-done((s32[1,1,256]{2,1,0:T(1,128)S(1)}, s32[1,1,256]{2,1,0:T(1,128)}, u32[]{:S(2)}) %copy-start.9) | copy-done | bytes 1048
  10.6 0.0 copy-start.10
  10.6 0.7 %copy-done.10 = s32[1,1,256]{2,1,0:T(1,128)S(1)} copy-done((s32[1,1,256]{2,1,0:T(1,128)S(1)}, s32[1,1,256]{2,1,0:T(1,128)}, u32[]{:S(2)}) %copy-start.10) | copy-done | bytes 1048
  11.3 0.0 copy-start.11
  11.3 0.7 %copy-done.11 = s32[1,1,256]{2,1,0:T(1,128)S(1)} copy-done((s32[1,1,256]{2,1,0:T(1,128)S(1)}, s32[1,1,256]{2,1,0:T(1,128)}, u32[]{:S(2)}) %copy-start.11) | copy-done | bytes 1048
  12.0 0.0 copy-start.12
  12.0 0.7 %copy-done.12 = f32[1,1,256]{2,1,0:T(1,128)S(1)} copy-done((f32[1,1,256]{2,1,0:T(1,128)S(1)}, f32[1,1,256]{2,1,0:T(1,128)}, u32[]{:S(2)}) %copy-start.12) | copy-done | bytes 1048
  12.6 0.0 copy-start.13
  12.6 0.7 %copy-done.13 = f32[1,1,32]{2,1,0:T(1,128)S(1)} copy-done((f32[1,1,32]{2,1,0:T(1,128)S(1)}, f32[1,1,32]{2,1,0:T(1,128)}, u32[]{:S(2)}) %copy-start.13) | copy-done | bytes 152
  13.3 31.1 %shard_map.149 = (f32[2,4,64,128]{3,2,1,0:T(8,128)S(1)}, f32[2,4,64,128]{3,2,1,0:T(8,128)S(1)}) custom-call(f32[2,4,64,128]{3,2,1,0:T(8,128)S(1)} %copy-done.4, f32[2,4,64,128]{3,2,1,0:T(8,128)S(1)} %copy-done.5, f32[2,4,64,128]{3,2,1,0:T(8,128)S(1)} %copy-done.6, f32[3,2,4,64,128]{4,3,2,1,0:T(8,128)S(1)} %copy-done, f32[3,2,4,64,128]{4,3,2,1,0:T(8,128)S(1)} %copy-done.1, ...), custom_call_target="tpu_custom_call" | custom-call | tf_op jit(solution)/shard_map/pallas_call | solution.py:506
  44.4 0.7 %copy.18 = f32[2,4,64,128]{3,2,1,0:T(8,128)} copy(f32[2,4,64,128]{3,2,1,0:T(8,128)S(1)} %get-tuple-element.4) | data formatting | bytes 524288
  45.1 0.7 %copy.19 = f32[2,4,64,128]{3,2,1,0:T(8,128)} copy(f32[2,4,64,128]{3,2,1,0:T(8,128)S(1)} %get-tuple-element.5) | data formatting | bytes 524288
Async XLA Ops:
  0.6 1.1 %copy-start = (f32[3,2,4,64,128]{4,3,2,1,0:T(8,128)S(1)}, f32[3,2,4,64,128]{4,3,2,1,0:T(8,128)}, u32[]{:S(2)}) copy-start(f32[3,2,4,64,128]{4,3,2,1,0:T(8,128)} %up_diag.1) | copy-start | bytes 2359300
  1.8 1.1 %copy-start.1 = (f32[3,2,4,64,128]{4,3,2,1,0:T(8,128)S(1)}, f32[3,2,4,64,128]{4,3,2,1,0:T(8,128)}, u32[]{:S(2)}) copy-start(f32[3,2,4,64,128]{4,3,2,1,0:T(8,128)} %up_cross.1) | copy-start | bytes 2359300
  2.9 1.1 %copy-start.2 = (f32[3,2,4,64,128]{4,3,2,1,0:T(8,128)S(1)}, f32[3,2,4,64,128]{4,3,2,1,0:T(8,128)}, u32[]{:S(2)}) copy-start(f32[3,2,4,64,128]{4,3,2,1,0:T(8,128)} %low_diag.1) | copy-start | bytes 2359300
  4.0 1.1 %copy-start.3 = (f32[3,2,4,64,128]{4,3,2,1,0:T(8,128)S(1)}, f32[3,2,4,64,128]{4,3,2,1,0:T(8,128)}, u32[]{:S(2)}) copy-start(f32[3,2,4,64,128]{4,3,2,1,0:T(8,128)} %low_cross.1) | copy-start | bytes 2359300
  5.2 0.9 %copy-start.4 = (f32[2,4,64,128]{3,2,1,0:T(8,128)S(1)}, f32[2,4,64,128]{3,2,1,0:T(8,128)}, u32[]{:S(2)}) copy-start(f32[2,4,64,128]{3,2,1,0:T(8,128)} %rhs.1) | copy-start | bytes 786436
  6.1 0.9 %copy-start.5 = (f32[2,4,64,128]{3,2,1,0:T(8,128)S(1)}, f32[2,4,64,128]{3,2,1,0:T(8,128)}, u32[]{:S(2)}) copy-start(f32[2,4,64,128]{3,2,1,0:T(8,128)} %cell_diag.1) | copy-start | bytes 786436
  7.1 0.9 %copy-start.6 = (f32[2,4,64,128]{3,2,1,0:T(8,128)S(1)}, f32[2,4,64,128]{3,2,1,0:T(8,128)}, u32[]{:S(2)}) copy-start(f32[2,4,64,128]{3,2,1,0:T(8,128)} %cell_cross.1) | copy-start | bytes 786436
  8.0 0.9 %copy-start.7 = (f32[2,4,64,128]{3,2,1,0:T(8,128)S(1)}, f32[2,4,64,128]{3,2,1,0:T(8,128)}, u32[]{:S(2)}) copy-start(f32[2,4,64,128]{3,2,1,0:T(8,128)} %spai_diag.1) | copy-start | bytes 786436
  9.0 0.9 %copy-start.8 = (f32[2,4,64,128]{3,2,1,0:T(8,128)S(1)}, f32[2,4,64,128]{3,2,1,0:T(8,128)}, u32[]{:S(2)}) copy-start(f32[2,4,64,128]{3,2,1,0:T(8,128)} %spai_cross.1) | copy-start | bytes 786436
  9.9 0.7 %copy-start.9 = (s32[1,1,256]{2,1,0:T(1,128)S(1)}, s32[1,1,256]{2,1,0:T(1,128)}, u32[]{:S(2)}) copy-start(s32[1,1,256]{2,1,0:T(1,128)} %perf_cell.1) | copy-start | bytes 3076
  10.6 0.7 %copy-start.10 = (s32[1,1,256]{2,1,0:T(1,128)S(1)}, s32[1,1,256]{2,1,0:T(1,128)}, u32[]{:S(2)}) copy-start(s32[1,1,256]{2,1,0:T(1,128)} %perf_owner.1) | copy-start | bytes 3076
  11.3 0.7 %copy-start.11 = (s32[1,1,256]{2,1,0:T(1,128)S(1)}, s32[1,1,256]{2,1,0:T(1,128)}, u32[]{:S(2)}) copy-start(s32[1,1,256]{2,1,0:T(1,128)} %perf_well.1) | copy-start | bytes 3076
  12.0 0.7 %copy-start.12 = (f32[1,1,256]{2,1,0:T(1,128)S(1)}, f32[1,1,256]{2,1,0:T(1,128)}, u32[]{:S(2)}) copy-start(f32[1,1,256]{2,1,0:T(1,128)} %perf_index.1) | copy-start | bytes 3076
  12.6 0.7 %copy-start.13 = (f32[1,1,32]{2,1,0:T(1,128)S(1)}, f32[1,1,32]{2,1,0:T(1,128)}, u32[]{:S(2)}) copy-start(f32[1,1,32]{2,1,0:T(1,128)} %storage.1) | copy-start | bytes 388

commit v2 on v1

--- a/solution.py
+++ b/solution.py
@@ -97,20 +97,18 @@
 
 def kernel(
     peers,
-    rhs,
-    cell_diag,
-    cell_cross,
-    up_diag,
-    up_cross,
-    low_diag,
-    low_cross,
-    spai_diag,
-    spai_cross,
-    perf_cell,
-    perf_owner,
-    perf_well,
-    perf_index,
-    storage,
+    *refs,
+):
+    inputs, (adjoint_out, residual_out) = (refs[:14], refs[14:16])
+    held, load_sem, refs = (refs[16:30], refs[30], refs[31:])
+    run(peers, inputs, held, load_sem, adjoint_out, residual_out, *refs)
+
+
+def run(
+    peers,
+    inputs,
+    held,
+    load_sem,
     adjoint_out,
     residual_out,
     basis,
@@ -136,6 +134,16 @@
     dots_send_sem,
     dots_recv_sem,
 ):
+    rhs, cell_diag, cell_cross, up_diag, up_cross, low_diag, low_cross = held[:7]
+    spai_diag, spai_cross, perf_cell, perf_owner, perf_well, perf_index, storage = held[7:]
+    loads = [pltpu.make_async_copy(inputs[k], held[k], load_sem.at[k]) for k in range(14)]
+    for k in (9, 10, 11, 12, 13, 0, 7, 8, 3, 4, 1, 2, 5, 6):
+        loads[k].start()
+
+    def ready(*which):
+        for k in which:
+            loads[k].wait()
+
     gx, gy = lax.axis_index("gx"), lax.axis_index("gy")
     everyone = peers * 2
     me = gx * 2 + gy
@@ -153,6 +161,7 @@
             barrier, 1, device_id={"gx": other // 2, "gy": other % 2}, device_id_type=MESH
         )
 
+    ready(9, 10, 11, 12, 13)
     cells = perf_cell[0]
     bucket_of = (perf_owner[0] & (RING - 1)) * owned + perf_well[0]
     row_of, layer_of = (cells // depth, cells % depth)
@@ -174,6 +183,7 @@
     bucket_of_layer = jnp.minimum(rows_dot(hot_layer, hot_bucket), 1.0).astype(BF16)
     layer_twice = jnp.concatenate([layer_of_bucket, layer_of_bucket], axis=0)
     bucket_twice = jnp.concatenate([bucket_of_layer, bucket_of_layer], axis=0)
+    ready(1)
     for c in range(2):
         for x in range(width):
             diag[c, x] = cell_diag[c, x] + extra[x * height : (x + 1) * height]
@@ -201,6 +211,7 @@
     first_lane, last_lane = (lane == 0, lane == depth - 1)
     first_row, last_row = (row == 0, row == height - 1)
 
+    ready(0, 7, 8)
     pl.semaphore_wait(barrier, everyone - 1)
 
     def vector(k):
@@ -281,6 +292,8 @@
             halo_copy(step, 1).start()
 
         f0, f1 = lift(width - 1)
+        if step == 0:
+            ready(3, 4)
         p0, p1 = block(up_diag, up_cross, ((0,), (width - 1,)), f0, f1)
         up_send[step, 0] = p0
         up_send[step, 1] = p1
@@ -329,6 +342,8 @@
         well_send[step, 6:8] = jnp.zeros((2, 128), F32)
         start_wells(step)
 
+        if step == 0:
+            ready(2, 5, 6)
         carry = None
         for x in range(width):
             f0, f1 = (lifted[step, 0, x], lifted[step, 1, x])
@@ -506,9 +521,11 @@
     return pl.pallas_call(
         functools.partial(kernel, peers),
         out_shape=[jax.ShapeDtypeStruct(rhs.shape, F32)] * 2,
-        in_specs=[vmem] * len(args),
+        in_specs=[pl.BlockSpec(memory_space=pl.ANY)] * len(args),
         out_specs=[vmem] * 2,
-        scratch_shapes=[
+        scratch_shapes=[pltpu.VMEM(a.shape, a.dtype) for a in args]
+        + [
+            pltpu.SemaphoreType.DMA((len(args),)),
             pltpu.VMEM((POWERS, 2, width, height, depth), F32),
             pltpu.VMEM((POWERS, 2, width, height, depth), F32),
             pltpu.VMEM((2, width, height, depth), F32),
@@ -533,7 +550,7 @@
             pltpu.SemaphoreType.DMA((everyone,)),
         ],
         compiler_params=pltpu.CompilerParams(
-            collective_id=0, has_side_effects=True, vmem_limit_bytes=40 * 1024 * 1024
+            collective_id=0, has_side_effects=True, vmem_limit_bytes=60 * 1024 * 1024
         ),
     )(*args)
 

time: 46.3 us -> 35.2 us (0.76)
  local copies, waits for them, and re-layouts: 14 us -> 2.42 us
  Pallas kernels: 31.1 us -> 32 us
    unnamed x30 -> x4, local copies, waits for them, and re-layouts: 14 us -> 2.42 us
    pallas_call x1, Pallas kernels: 31.1 us -> 32 us  [shards(): pl.pallas_call(functools.partial(kernel, peers), out_shape=[jax.ShapeDtyp...]
where the time goes in v2:
time: 35.2 us; the launch traced here: 35 us
  Pallas kernels  32 us (91%)
  local copies, waits for them, and re-layouts  2.42 us (7%)
  between operations  0.65 us (2%)
    pallas_call x1, Pallas kernels, shards(): pl.pallas_call(functools.partial(kernel, peers), out_shape=[jax.ShapeDtyp...  32 us
    unnamed x4, local copies, waits for them, and re-layouts  2.42 us

profile of v2, /device:TPU:0, one launch (start us, length us, event | category | flops | bytes accessed | tf_op | source)
XLA Modules:
  0.0 35.0 jit_solution(11051431824693272717)
XLA Ops:
  0.6 32.0 %shard_map.149 = (f32[2,4,64,128]{3,2,1,0:T(8,128)}, f32[2,4,64,128]{3,2,1,0:T(8,128)}) custom-call(f32[2,4,64,128]{3,2,1,0:T(8,128)} %refs_0_.1, f32[2,4,64,128]{3,2,1,0:T(8,128)} %refs_1_.1, f32[2,4,64,128]{3,2,1,0:T(8,128)} %refs_2_.1, f32[3,2,4,64,128]{4,3,2,1,0:T(8,128)} %refs_3_.1, f32[3,2,4,64,128]{4,3,2,1,0:T(8,128)} %refs_4_.1, ...), custom_call_target="tpu_custom_call" | custom-call | tf_op jit(solution)/shard_map/pallas_call | solution.py:521
  32.6 0.0 copy-start
  32.6 1.7 %copy.18 = f32[2,4,64,128]{3,2,1,0:T(8,128)} copy(f32[2,4,64,128]{3,2,1,0:T(8,128)} %get-tuple-element.4) | data formatting | bytes 524288
  34.3 0.0 copy-done
  34.3 0.7 %copy.19 = f32[2,4,64,128]{3,2,1,0:T(8,128)} copy(f32[2,4,64,128]{3,2,1,0:T(8,128)S(1)} %copy-done) | data formatting | bytes 524288
Async XLA Ops:
  32.6 1.7 %copy-start = (f32[2,4,64,128]{3,2,1,0:T(8,128)S(1)}, f32[2,4,64,128]{3,2,1,0:T(8,128)}, u32[]{:S(2)}) copy-start(f32[2,4,64,128]{3,2,1,0:T(8,128)} %get-tuple-element.5) | copy-start | bytes 786436

commit v3 on v2

--- a/solution.py
+++ b/solution.py
@@ -13,6 +13,7 @@
 SHIFT = 1.0
 RING = 8
 REACH = 4
+PIECES = 2
 F32 = jnp.float32
 BF16 = jnp.bfloat16
 
@@ -126,6 +127,7 @@
     well_send,
     well_recv,
     dots,
+    packed,
     dots_all,
     halo_send_sem,
     halo_recv_sem,
@@ -137,7 +139,7 @@
     rhs, cell_diag, cell_cross, up_diag, up_cross, low_diag, low_cross = held[:7]
     spai_diag, spai_cross, perf_cell, perf_owner, perf_well, perf_index, storage = held[7:]
     loads = [pltpu.make_async_copy(inputs[k], held[k], load_sem.at[k]) for k in range(14)]
-    for k in (9, 10, 11, 12, 13, 0, 7, 8, 3, 4, 1, 2, 5, 6):
+    for k in (0, 7, 8, 9, 10, 11, 12, 13, 3, 4, 1, 2, 5, 6):
         loads[k].start()
 
     def ready(*which):
@@ -160,6 +162,114 @@
         pl.semaphore_signal(
             barrier, 1, device_id={"gx": other // 2, "gy": other % 2}, device_id_type=MESH
         )
+
+    lane = lax.broadcasted_iota(jnp.int32, (height, depth), 1)
+    row = lax.broadcasted_iota(jnp.int32, (height, depth), 0)
+    first_lane, last_lane = (lane == 0, lane == depth - 1)
+    first_row, last_row = (row == 0, row == height - 1)
+
+    ready(0, 7, 8)
+    pl.semaphore_wait(barrier, everyone - 1)
+
+    def vector(k):
+        return rhs if k == 0 else basis.at[k - 1]
+
+    def start_wells(step):
+        for k in range(2 * REACH + 1):
+            if k == REACH:
+                continue
+            away = REACH - k
+
+            @pl.when((gx + away >= 0) & (gx + away < peers))
+            def _():
+                pltpu.make_async_remote_copy(
+                    src_ref=well_send.at[step],
+                    dst_ref=well_recv.at[step, k],
+                    send_sem=well_send_sem.at[step, k],
+                    recv_sem=well_recv_sem.at[step, k],
+                    device_id={"gx": gx + away},
+                    device_id_type=MESH,
+                ).start()
+
+    def well_copy(step, k):
+        return pltpu.make_async_remote_copy(
+            src_ref=well_send.at[step],
+            dst_ref=well_recv.at[step, k],
+            send_sem=well_send_sem.at[step, k],
+            recv_sem=well_recv_sem.at[step, k],
+            device_id={"gx": gx},
+            device_id_type=MESH,
+        )
+
+    def halo_copy(step, kind):
+        way, piece = divmod(kind, PIECES)
+        at = pl.ds(piece * (height // PIECES), height // PIECES)
+        if way == 0:
+            src, dst, target = (up_send.at[step, :, at], up_recv.at[step, :, at], {"gx": gx + 1})
+        elif way == 1:
+            src, dst, target = (
+                lifted.at[step, :, 0, at],
+                down_recv.at[step, :, at],
+                {"gx": gx - 1},
+            )
+        else:
+            src, dst, target = (y_send.at[step], y_recv.at[step], {"gy": 1 - gy})
+        return pltpu.make_async_remote_copy(
+            src_ref=src,
+            dst_ref=dst,
+            send_sem=halo_send_sem.at[step, kind],
+            recv_sem=halo_recv_sem.at[step, kind],
+            device_id=target,
+            device_id_type=MESH,
+        )
+
+    def block(diag_ref, cross_ref, at, f0, f1):
+        d0, d1 = (diag_ref[(*at[0], 0, *at[1])], diag_ref[(*at[0], 1, *at[1])])
+        c0, c1 = (cross_ref[(*at[0], 0, *at[1])], cross_ref[(*at[0], 1, *at[1])])
+        return (d0 * f0 + c1 * f1, c0 * f0 + d1 * f1)
+
+    def add_dots(k):
+        sums = [jnp.zeros((8, depth), F32) for _ in range(k + 1)]
+        for c in range(2):
+            for x in range(width):
+                last = vector(k)[c, x]
+                for j in range(k + 1):
+                    other = last if j == k else vector(j)[c, x]
+                    sums[j] += jnp.sum((last * other).reshape(height // 8, 8, depth), axis=0)
+        for j in range(k + 1):
+            at = k * (k + 1) // 2 + j
+            dots[at : at + 1, :] = jnp.sum(sums[j], axis=0, keepdims=True)
+
+    def lift(step, x, at):
+        source = vector(step)
+        f0, f1 = block(spai_diag, spai_cross, ((), (x, at)), source[0, x, at], source[1, x, at])
+        lifted[step, 0, x, at] = f0
+        lifted[step, 1, x, at] = f1
+        return f0, f1
+
+    def start_planes(step, piece):
+        @pl.when(gx > 0)
+        def _():
+            halo_copy(step, PIECES + piece).start()
+
+        @pl.when(gx < peers - 1)
+        def _():
+            halo_copy(step, piece).start()
+
+    def send_planes(step, piece):
+        at = slice(piece * (height // PIECES), (piece + 1) * (height // PIECES))
+        lift(step, 0, at)
+        f0, f1 = lift(step, width - 1, at)
+        if step == 0 and piece == 0:
+            ready(3, 4)
+        p0, p1 = block(up_diag, up_cross, ((0,), (width - 1, at)), f0, f1)
+        up_send[step, 0, at] = p0
+        up_send[step, 1, at] = p1
+        if piece == 0:
+            start_planes(step, piece)
+
+    for piece in range(PIECES):
+        send_planes(0, piece)
 
     ready(9, 10, 11, 12, 13)
     cells = perf_cell[0]
@@ -206,104 +316,10 @@
         same = (here < 5) & (there < 5) & (here == there + away)
         mask[k] = same.astype(F32)
 
-    lane = lax.broadcasted_iota(jnp.int32, (height, depth), 1)
-    row = lax.broadcasted_iota(jnp.int32, (height, depth), 0)
-    first_lane, last_lane = (lane == 0, lane == depth - 1)
-    first_row, last_row = (row == 0, row == height - 1)
-
-    ready(0, 7, 8)
-    pl.semaphore_wait(barrier, everyone - 1)
-
-    def vector(k):
-        return rhs if k == 0 else basis.at[k - 1]
-
-    def start_wells(step):
-        for k in range(2 * REACH + 1):
-            if k == REACH:
-                continue
-            away = REACH - k
-
-            @pl.when((gx + away >= 0) & (gx + away < peers))
-            def _():
-                pltpu.make_async_remote_copy(
-                    src_ref=well_send.at[step],
-                    dst_ref=well_recv.at[step, k],
-                    send_sem=well_send_sem.at[step, k],
-                    recv_sem=well_recv_sem.at[step, k],
-                    device_id={"gx": gx + away},
-                    device_id_type=MESH,
-                ).start()
-
-    def well_copy(step, k):
-        return pltpu.make_async_remote_copy(
-            src_ref=well_send.at[step],
-            dst_ref=well_recv.at[step, k],
-            send_sem=well_send_sem.at[step, k],
-            recv_sem=well_recv_sem.at[step, k],
-            device_id={"gx": gx},
-            device_id_type=MESH,
-        )
-
-    def halo_copy(step, kind):
-        src, dst, target = [
-            (up_send.at[step], up_recv.at[step], {"gx": gx + 1}),
-            (lifted.at[step, :, 0], down_recv.at[step], {"gx": gx - 1}),
-            (y_send.at[step], y_recv.at[step], {"gy": 1 - gy}),
-        ][kind]
-        return pltpu.make_async_remote_copy(
-            src_ref=src,
-            dst_ref=dst,
-            send_sem=halo_send_sem.at[step, kind],
-            recv_sem=halo_recv_sem.at[step, kind],
-            device_id=target,
-            device_id_type=MESH,
-        )
-
-    def block(diag_ref, cross_ref, at, f0, f1):
-        d0, d1 = (diag_ref[(*at[0], 0, *at[1])], diag_ref[(*at[0], 1, *at[1])])
-        c0, c1 = (cross_ref[(*at[0], 0, *at[1])], cross_ref[(*at[0], 1, *at[1])])
-        return (d0 * f0 + c1 * f1, c0 * f0 + d1 * f1)
-
-    def add_dots(k):
-        sums = [jnp.zeros((8, depth), F32) for _ in range(k + 1)]
-        for c in range(2):
-            for x in range(width):
-                last = vector(k)[c, x]
-                for j in range(k + 1):
-                    other = last if j == k else vector(j)[c, x]
-                    sums[j] += jnp.sum((last * other).reshape(height // 8, 8, depth), axis=0)
-        for j in range(k + 1):
-            at = k * (k + 1) // 2 + j
-            dots[at : at + 1, :] = jnp.sum(sums[j], axis=0, keepdims=True)
-
     for step in range(POWERS):
         source = vector(step)
-
-        def lift(x):
-            f0, f1 = block(spai_diag, spai_cross, ((), (x,)), source[0, x], source[1, x])
-            lifted[step, 0, x] = f0
-            lifted[step, 1, x] = f1
-            return f0, f1
-
-        lift(0)
-
-        @pl.when(gx > 0)
-        def _():
-            halo_copy(step, 1).start()
-
-        f0, f1 = lift(width - 1)
-        if step == 0:
-            ready(3, 4)
-        p0, p1 = block(up_diag, up_cross, ((0,), (width - 1,)), f0, f1)
-        up_send[step, 0] = p0
-        up_send[step, 1] = p1
-
-        @pl.when(gx < peers - 1)
-        def _():
-            halo_copy(step, 0).start()
-
         for x in range(1, width - 1):
-            lift(x)
+            lift(step, x, slice(0, height))
 
         @pl.when(gy == 0)
         def _():
@@ -325,7 +341,7 @@
                 for c in range(2):
                     y_send[step, c * width + x : c * width + x + 1] = lifted[step, c, x, 0:1]
 
-        halo_copy(step, 2).start()
+        halo_copy(step, 2 * PIECES).start()
 
         for c in range(2):
             field = lifted[step, c].reshape(rows, depth)
@@ -341,6 +357,8 @@
         well_send[step, 5:6] = weight_sums[:, 128:]
         well_send[step, 6:8] = jnp.zeros((2, 128), F32)
         start_wells(step)
+        for piece in range(1, PIECES):
+            start_planes(step, piece)
 
         if step == 0:
             ready(2, 5, 6)
@@ -405,7 +423,7 @@
             for x in range(width):
                 basis[step, c, x] -= taken[x * height : (x + 1) * height]
 
-        halo_copy(step, 2).wait_recv()
+        halo_copy(step, 2 * PIECES).wait_recv()
 
         @pl.when(gy == 0)
         def _():
@@ -423,27 +441,37 @@
                     at = c * width + x
                     basis[step, c, x, 0:1] -= y_recv[step, at : at + 1]
 
-        @pl.when(gx > 0)
-        def _():
-            halo_copy(step, 0).wait_recv()
-            for c in range(2):
-                basis[step, c, 0] -= up_recv[step, c]
-
-        @pl.when(gx < peers - 1)
-        def _():
-            halo_copy(step, 1).wait_recv()
-            x = width - 1
-            f0, f1 = (down_recv[step, 0], down_recv[step, 1])
-            b0, b1 = block(low_diag, low_cross, ((0,), (x,)), f0, f1)
-            basis[step, 0, x] -= b0
-            basis[step, 1, x] -= b1
+        for piece in range(PIECES):
+            at = slice(piece * (height // PIECES), (piece + 1) * (height // PIECES))
+
+            @pl.when(gx > 0)
+            def _():
+                halo_copy(step, piece).wait_recv()
+                for c in range(2):
+                    basis[step, c, 0, at] -= up_recv[step, c, at]
+
+            @pl.when(gx < peers - 1)
+            def _():
+                halo_copy(step, PIECES + piece).wait_recv()
+                x = width - 1
+                f0, f1 = (down_recv[step, 0, at], down_recv[step, 1, at])
+                b0, b1 = block(low_diag, low_cross, ((0,), (x, at)), f0, f1)
+                basis[step, 0, x, at] -= b0
+                basis[step, 1, x, at] -= b1
+
+            if step < POWERS - 1:
+                send_planes(step + 1, piece)
 
     add_dots(POWERS)
     dots[15:16, :] = jnp.zeros((1, depth), F32)
+    on_lane = lax.broadcasted_iota(jnp.int32, (16, depth), 1)
+    on_lane = on_lane == lax.broadcasted_iota(jnp.int32, (16, depth), 0)
+    sums = jnp.sum(dots[...], axis=1, keepdims=True)
+    packed[...] = jnp.sum(jnp.where(on_lane, sums, 0.0), axis=0, keepdims=True)
 
     def dots_copy(index, other):
         return pltpu.make_async_remote_copy(
-            src_ref=dots,
+            src_ref=packed,
             dst_ref=dots_all.at[index],
             send_sem=dots_send_sem.at[index],
             recv_sem=dots_recv_sem.at[index],
@@ -454,18 +482,18 @@
     for step in range(1, everyone):
         other = lax.rem(me + step, everyone)
         pltpu.make_async_remote_copy(
-            src_ref=dots,
+            src_ref=packed,
             dst_ref=dots_all.at[me],
             send_sem=dots_send_sem.at[step],
             recv_sem=dots_recv_sem.at[me],
             device_id={"gx": other // 2, "gy": other % 2},
             device_id_type=MESH,
         ).start()
-    dots_all[me] = dots[...]
+    dots_all[me] = packed[...]
     for step in range(1, everyone):
         other = lax.rem(me + step, everyone)
         dots_copy(other, other).wait_recv()
-    gathered = jnp.sum(dots_all[...], axis=0)
+    gathered = jnp.where(on_lane, jnp.sum(dots_all[...], axis=0), 0.0)
     gathered = jnp.broadcast_to(jnp.sum(gathered, axis=1, keepdims=True), gathered.shape)
     gram = {}
     for k in range(POWERS + 1):
@@ -486,15 +514,17 @@
 
     for step in range(POWERS):
 
-        @pl.when(gx < peers - 1)
-        def _():
-            halo_copy(step, 0).wait_send()
-
-        @pl.when(gx > 0)
-        def _():
-            halo_copy(step, 1).wait_send()
-
-        halo_copy(step, 2).wait_send()
+        for piece in range(PIECES):
+
+            @pl.when(gx < peers - 1)
+            def _():
+                halo_copy(step, piece).wait_send()
+
+            @pl.when(gx > 0)
+            def _():
+                halo_copy(step, PIECES + piece).wait_send()
+
+        halo_copy(step, 2 * PIECES).wait_send()
         for k in range(2 * REACH + 1):
             if k == REACH:
                 continue
@@ -506,6 +536,17 @@
 
     for step in range(1, everyone):
         dots_copy(step, me).wait_send()
+
+
+def store(first, second, first_out, second_out, sem):
+    copies = [
+        pltpu.make_async_copy(first, first_out, sem.at[0]),
+        pltpu.make_async_copy(second, second_out, sem.at[1]),
+    ]
+    for copy in copies:
+        copy.start()
+    for copy in copies:
+        copy.wait()
 
 
 def shards(peers, *args):
@@ -518,7 +559,7 @@
     plane = (POWERS, 2, height, depth)
     wells = 2 * REACH + 1
     vmem = pl.BlockSpec(memory_space=pltpu.VMEM)
-    return pl.pallas_call(
+    results = pl.pallas_call(
         functools.partial(kernel, peers),
         out_shape=[jax.ShapeDtypeStruct(rhs.shape, F32)] * 2,
         in_specs=[pl.BlockSpec(memory_space=pl.ANY)] * len(args),
@@ -541,9 +582,10 @@
             pltpu.VMEM((POWERS, 8, 128), F32),
             pltpu.VMEM((POWERS, wells, 8, 128), F32),
             pltpu.VMEM((16, depth), F32),
-            pltpu.VMEM((everyone, 16, depth), F32),
-            pltpu.SemaphoreType.DMA((POWERS, 3)),
-            pltpu.SemaphoreType.DMA((POWERS, 3)),
+            pltpu.VMEM((1, depth), F32),
+            pltpu.VMEM((everyone, 1, depth), F32),
+            pltpu.SemaphoreType.DMA((POWERS, 2 * PIECES + 1)),
+            pltpu.SemaphoreType.DMA((POWERS, 2 * PIECES + 1)),
             pltpu.SemaphoreType.DMA((POWERS, wells)),
             pltpu.SemaphoreType.DMA((POWERS, wells)),
             pltpu.SemaphoreType.DMA((everyone,)),
@@ -553,6 +595,14 @@
             collective_id=0, has_side_effects=True, vmem_limit_bytes=60 * 1024 * 1024
         ),
     )(*args)
+    anywhere = pl.BlockSpec(memory_space=pl.ANY)
+    return pl.pallas_call(
+        store,
+        out_shape=[jax.ShapeDtypeStruct(rhs.shape, F32)] * 2,
+        in_specs=[vmem] * 2,
+        out_specs=[anywhere] * 2,
+        scratch_shapes=[pltpu.SemaphoreType.DMA((2,))],
+    )(*results)
 
 
 def solution(mesh):

time: 35.2 us -> 33.1 us (0.940)
  local copies, waits for them, and re-layouts: 2.42 us -> 0 us
  Pallas kernels: 32 us -> 32.4 us
    unnamed x4 -> x0, local copies, waits for them, and re-layouts: 2.42 us -> none
    pallas_call x0 -> x1, Pallas kernels: none -> 1.83 us  [shards(): pl.pallas_call(store, out_shape=[jax.ShapeDtypeStruct(rhs.shape, F32)] *...]
    pallas_call x1, Pallas kernels: 32 us -> 30.5 us  [shards(): pl.pallas_call(functools.partial(kernel, peers), out_shape=[jax.ShapeDtyp...]
where the time goes in v3:
time: 33.1 us; the launch traced here: 33 us
  Pallas kernels  32.4 us (98%)
  between operations  0.64 us (2%)
    pallas_call x1, Pallas kernels, shards(): pl.pallas_call(functools.partial(kernel, peers), out_shape=[jax.ShapeDtyp...  30.5 us
    pallas_call x1, Pallas kernels, shards(): pl.pallas_call(store, out_shape=[jax.ShapeDtypeStruct(rhs.shape, F32)] *...  1.83 us

profile of v3, /device:TPU:0, one launch (start us, length us, event | category | flops | bytes accessed | tf_op | source)
XLA Modules:
  0.0 33.0 jit_solution(16181578631654408980)
XLA Ops:
  0.6 30.5 %shard_map.149 = (f32[2,4,64,128]{3,2,1,0:T(8,128)}, f32[2,4,64,128]{3,2,1,0:T(8,128)}) custom-call(f32[2,4,64,128]{3,2,1,0:T(8,128)} %refs_0_.1, f32[2,4,64,128]{3,2,1,0:T(8,128)} %refs_1_.1, f32[2,4,64,128]{3,2,1,0:T(8,128)} %refs_2_.1, f32[3,2,4,64,128]{4,3,2,1,0:T(8,128)} %refs_3_.1, f32[3,2,4,64,128]{4,3,2,1,0:T(8,128)} %refs_4_.1, ...), custom_call_target="tpu_custom_call" | custom-call | tf_op jit(solution)/shard_map/pallas_call | solution.py:562
  31.2 1.8 %shard_map.150 = (f32[2,4,64,128]{3,2,1,0:T(8,128)}, f32[2,4,64,128]{3,2,1,0:T(8,128)}) custom-call(f32[2,4,64,128]{3,2,1,0:T(8,128)} %get-tuple-element.4.first, f32[2,4,64,128]{3,2,1,0:T(8,128)} %get-tuple-element.5.second), custom_call_target="tpu_custom_call" | custom-call | tf_op jit(solution)/shard_map/pallas_call | solution.py:599

commit v4 on v3

--- a/solution.py
+++ b/solution.py
@@ -157,11 +157,23 @@
 
     well_recv[...] = jnp.zeros_like(well_recv)
     barrier = pltpu.get_barrier_semaphore()
-    for step in range(1, everyone):
-        other = lax.rem(me + step, everyone)
-        pl.semaphore_signal(
-            barrier, 1, device_id={"gx": other // 2, "gy": other % 2}, device_id_type=MESH
-        )
+    chained = REACH <= peers <= 2 * REACH
+    if chained:
+        pl.semaphore_signal(barrier, 1, device_id={"gy": 1 - gy}, device_id_type=MESH)
+        for away in range(-REACH, REACH + 1):
+            if away == 0:
+                continue
+
+            @pl.when((gx + away >= 0) & (gx + away < peers))
+            def _():
+                pl.semaphore_signal(barrier, 1, device_id={"gx": gx + away}, device_id_type=MESH)
+
+    else:
+        for step in range(1, everyone):
+            other = lax.rem(me + step, everyone)
+            pl.semaphore_signal(
+                barrier, 1, device_id={"gx": other // 2, "gy": other % 2}, device_id_type=MESH
+            )
 
     lane = lax.broadcasted_iota(jnp.int32, (height, depth), 1)
     row = lax.broadcasted_iota(jnp.int32, (height, depth), 0)
@@ -169,7 +181,13 @@
     first_row, last_row = (row == 0, row == height - 1)
 
     ready(0, 7, 8)
-    pl.semaphore_wait(barrier, everyone - 1)
+    if chained:
+        near = 1
+        for away in range(1, REACH + 1):
+            near = near + (gx + peers - away) // peers + 1 - (gx + away) // peers
+        pl.semaphore_wait(barrier, near)
+    else:
+        pl.semaphore_wait(barrier, everyone - 1)
 
     def vector(k):
         return rhs if k == 0 else basis.at[k - 1]

time: 33.1 us -> 32.3 us (0.976)
  Pallas kernels: 32.4 us -> 31.5 us
    pallas_call x1, Pallas kernels: 30.5 us -> 29.7 us  [shards(): pl.pallas_call(functools.partial(kernel, peers), out_shape=[jax.ShapeDtyp...]
where the time goes in v4:
time: 32.3 us; the launch traced here: 32.2 us
  Pallas kernels  31.5 us (98%)
  between operations  0.64 us (2%)
    pallas_call x1, Pallas kernels, shards(): pl.pallas_call(functools.partial(kernel, peers), out_shape=[jax.ShapeDtyp...  29.7 us
    pallas_call x1, Pallas kernels, shards(): pl.pallas_call(store, out_shape=[jax.ShapeDtypeStruct(rhs.shape, F32)] *...  1.83 us

profile of v4, /device:TPU:0, one launch (start us, length us, event | category | flops | bytes accessed | tf_op | source)
XLA Modules:
  0.0 32.2 jit_solution(5293261541523427765)
XLA Ops:
  0.6 29.7 %shard_map.149 = (f32[2,4,64,128]{3,2,1,0:T(8,128)}, f32[2,4,64,128]{3,2,1,0:T(8,128)}) custom-call(f32[2,4,64,128]{3,2,1,0:T(8,128)} %refs_0_.1, f32[2,4,64,128]{3,2,1,0:T(8,128)} %refs_1_.1, f32[2,4,64,128]{3,2,1,0:T(8,128)} %refs_2_.1, f32[3,2,4,64,128]{4,3,2,1,0:T(8,128)} %refs_3_.1, f32[3,2,4,64,128]{4,3,2,1,0:T(8,128)} %refs_4_.1, ...), custom_call_target="tpu_custom_call" | custom-call | tf_op jit(solution)/shard_map/pallas_call | solution.py:580
  30.4 1.8 %shard_map.150 = (f32[2,4,64,128]{3,2,1,0:T(8,128)}, f32[2,4,64,128]{3,2,1,0:T(8,128)}) custom-call(f32[2,4,64,128]{3,2,1,0:T(8,128)} %get-tuple-element.4.first, f32[2,4,64,128]{3,2,1,0:T(8,128)} %get-tuple-element.5.second), custom_call_target="tpu_custom_call" | custom-call | tf_op jit(solution)/shard_map/pallas_call | solution.py:617
